TPU v7x, 128 devices: a whole 4x4x4 slice. The times are simulated.
128 devices in a mesh: block: 8 (over x_lo, y), dp: 16 (over x_hi, z, core).
Axes of the slice: x: 4 (x_hi: 2, x_lo: 2; x = x_hi * 2 + x_lo), y: 4, z: 4, core: 2. Of those that a mesh axis runs over, the one named last changes fastest.
Arguments:
- inputs: bfloat16 [16, 3072, 1536], P('dp', 'block'), may hold values from -32 to 32
- w_query: bfloat16 [1536, 1536], replicated, may hold values from -0.25 to 0.25
- w_key: bfloat16 [1536, 1536], replicated, may hold values from -0.25 to 0.25
- w_value: bfloat16 [1536, 1536], replicated, may hold values from -0.15625 to 0.15625
- out_grad: bfloat16 [16, 3072, 1536], P('dp', 'block'), may hold values from -6 to 6
Outputs:
- input_grad: bfloat16 [16, 3072, 1536], P('dp', 'block')
- grad_query: float32 [1536, 1536], P('block')
- grad_key: float32 [1536, 1536], P('block')
- grad_value: float32 [1536, 1536], P('block')
All inputs are finite; a program needn't handle non-finite values.
Results may differ from a plain program's by a relative error of at most 0.03.
Values may be sent and summed in bfloat16 or wider, within the bound.
No kernel may reach another device: no remote copies, remote signals or barrier semaphores. Data moves between devices by JAX's collectives and lax.ppermute only.
A program may use at most 192 MiB of HBM per device.

v0:
```python
import jax
import jax.numpy as jnp
from jax import lax
from jax.experimental import pallas as pl
from jax.experimental.pallas import tpu as pltpu
from jax.sharding import Mesh, PartitionSpec as P

D = 1536
HEADS = 12
HEAD = 128
GROUP = HEADS // 4
COLS = GROUP * 3 * HEAD
SCALE = HEAD ** (-0.5)
LOG2E = 1.4426950408889634
FIRST = 2**40
BF = jnp.bfloat16
F32 = jnp.float32


def dot(a, b, ca, cb):
    return lax.dot_general(a, b, (((ca,), (cb,)), ((), ())), preferred_element_type=F32)


def attention_kernel(
    tok, nz, place_ref, bias_ref, q_ref, kv_ref, halo_ref, dout_ref, turned_ref,
    dq_ref, dkv_ref, dhalo_ref, give_ref, keep_ref, low_ref, high_ref,
    acc_ref, held_ref, grad_ref, sem_ref,
):
    step = pl.program_id(0)
    fetch = pltpu.make_async_copy(turned_ref, held_ref, sem_ref)

    @pl.when(step == 0)
    def _():
        fetch.start()

    bias = bias_ref[0, 0]
    zero = jnp.zeros((tok, HEAD), BF)

    def first(i):
        here = slice(i * tok, (i + 1) * tok)
        kv = kv_ref[max(i - 2, 0) * tok : (i + 1) * tok, :]
        if i < 2:
            kv = jnp.concatenate([halo_ref[i * tok : 2 * tok, :], kv], axis=0)
        qd = jnp.concatenate(
            [
                jnp.concatenate([q_ref[here, :], zero], axis=1),
                jnp.concatenate([zero, dout_ref[here, :]], axis=1),
            ],
            axis=0,
        )
        return kv, qd, dot(kv, qd, 1, 1)

    def second(i, kv, qd, both):
        s = both[:, :tok]
        dp = both[:, tok:]
        if i < 2:
            edge = (2 - i) * tok
            s = jnp.concatenate([s[:edge] + bias, s[edge:]], axis=0)
        peak = jnp.max(s, axis=0, keepdims=True) * (SCALE * LOG2E)
        e = jnp.exp2(s * (SCALE * LOG2E) - peak)
        p = e * (1.0 / jnp.sum(e, axis=0, keepdims=True))
        delta = jnp.sum(p * dp, axis=0, keepdims=True)
        ds = (p * (dp - delta)).astype(BF)
        dkv = dot(jnp.concatenate([ds, p.astype(BF)], axis=1), qd, 1, 0)
        for j in range(3):
            rows = slice((i + j) * tok, (i + j + 1) * tok)
            part = dkv[j * tok : (j + 1) * tok]
            if i == 0 or j == 2:
                acc_ref[rows, :] = part
            else:
                acc_ref[rows, :] += part
        dq = dot(kv[:, :HEAD], ds, 0, 0).T * SCALE
        dq_ref[i * tok : (i + 1) * tok, :] = dq.astype(BF)

    ahead = first(0)
    for i in range(4):
        now = ahead
        if i < 3:
            ahead = first(i + 1)
        second(i, *now)
    dkv_ref[:, :HEAD] = (acc_ref[2 * tok :, :HEAD] * SCALE).astype(BF)
    dkv_ref[:, HEAD:] = acc_ref[2 * tok :, HEAD:].astype(BF)
    dhalo_ref[:, :HEAD] = (acc_ref[: 2 * tok, :HEAD] * SCALE).astype(BF)
    dhalo_ref[:, HEAD:] = acc_ref[: 2 * tok, HEAD:].astype(BF)

    @pl.when(step == 0)
    def _():
        fetch.wait()
        low_ref[...] = held_ref[: D // 2, 2 * tok :]
        high_ref[...] = held_ref[D // 2 :, 2 * tok :]

    grad_ref[:, : 2 * HEAD] = dot(held_ref[...], dkv_ref[...], 1, 0)
    grad_ref[:, 2 * HEAD :] = dot(held_ref[...], dq_ref[...], 1, 0)
    fine = D // 8 // nz
    for out_ref, side in ((give_ref, 1 - place_ref[0]), (keep_ref, place_ref[0])):
        for steps in range(nz):
            for y in range(4):
                start = side * (D // 2) + (y * nz + lax.rem(place_ref[1] + steps, nz)) * fine
                rows = pl.ds(pl.multiple_of(start, 16), fine)
                out_ref[steps, y] = grad_ref[rows, :].astype(BF)


def attention(place, bias, q, kv, halo, dout, turned, nz):
    tok = q.shape[0] // 4
    one = pl.BlockSpec((4 * tok, HEAD), lambda h, place: (0, h))
    two = pl.BlockSpec((4 * tok, 2 * HEAD), lambda h, place: (0, h))
    edge = pl.BlockSpec((2 * tok, 2 * HEAD), lambda h, place: (0, h))
    corner = pl.BlockSpec((D // 2, 2 * tok), lambda h, place: (0, 0))
    shape = (nz, 4, D // 8 // nz, COLS)
    slabs = pl.BlockSpec(shape[:3] + (3 * HEAD,), lambda h, place: (0, 0, 0, h))
    made = lambda shape: jax.ShapeDtypeStruct(shape, BF)
    return pl.pallas_call(
        lambda *refs: attention_kernel(tok, nz, *refs),
        grid_spec=pltpu.PrefetchScalarGridSpec(
            num_scalar_prefetch=1,
            grid=(GROUP,),
            in_specs=[
                pl.BlockSpec(memory_space=pltpu.SMEM), one, two, edge, one,
                pl.BlockSpec(memory_space=pl.ANY),
            ],
            out_specs=[one, two, edge, slabs, slabs, corner, corner],
            scratch_shapes=[
                pltpu.VMEM((6 * tok, 2 * HEAD), F32),
                pltpu.VMEM((D, 4 * tok), BF),
                pltpu.VMEM((D, 3 * HEAD), F32),
                pltpu.SemaphoreType.DMA,
            ],
        ),
        out_shape=[
            made(q.shape), made(kv.shape), made(halo.shape), made(shape), made(shape),
            made((D // 2, 2 * tok)), made((D // 2, 2 * tok)),
        ],
        compiler_params=pltpu.CompilerParams(vmem_limit_bytes=60 * 1024 * 1024),
        cost_estimate=pl.CostEstimate(
            flops=2 * 5 * 4 * GROUP * 3 * tok * tok * HEAD * 2 + 8 * tok * D * COLS,
            bytes_accessed=24 * kv.size,
            transcendentals=4 * GROUP * 3 * tok * tok,
        ),
    )(place, bias, q, kv, halo, dout, turned)


def pick_kernel(place_ref, query_ref, key_ref, value_ref, q_ref, kv_ref):
    q_ref[...] = query_ref[...]
    kv_ref[:, :HEAD] = key_ref[...]
    kv_ref[:, HEAD:] = value_ref[...]


def pick_weights(index, w_query, w_key, w_value):
    piece = pl.BlockSpec((D, HEAD), lambda h, place: (0, place[0] * GROUP + h))
    return pl.pallas_call(
        pick_kernel,
        grid_spec=pltpu.PrefetchScalarGridSpec(
            num_scalar_prefetch=1,
            grid=(GROUP,),
            in_specs=[piece, piece, piece],
            out_specs=[
                pl.BlockSpec((D, HEAD), lambda h, place: (0, h)),
                pl.BlockSpec((D, 2 * HEAD), lambda h, place: (0, h)),
            ],
        ),
        out_shape=[
            jax.ShapeDtypeStruct((D, GROUP * HEAD), BF),
            jax.ShapeDtypeStruct((D, 2 * GROUP * HEAD), BF),
        ],
        compiler_params=pltpu.CompilerParams(vmem_limit_bytes=60 * 1024 * 1024),
        cost_estimate=pl.CostEstimate(
            flops=FIRST, bytes_accessed=4 * D * COLS, transcendentals=0
        ),
    )(index.reshape(1), w_query, w_key, w_value)


def place_kernel(split, place_ref, a_ref, b_ref, wkv_ref, wq_ref, *refs):
    t_ref, kv_ref, q_ref, block_ref = refs[-4:]
    step = pl.program_id(0)

    @pl.when(step == 0)
    def _():
        if split:
            half = a_ref.shape[0]
            block_ref[:half, :] = a_ref[...]
            block_ref[half:, :] = b_ref[...]
        else:
            block_ref[...] = a_ref[...]

            @pl.when(place_ref[1] == 0)
            def _():
                block_ref[...] = b_ref[...]

    block = block_ref[...]
    kv_ref[...] = dot(block, wkv_ref[...], 1, 0).astype(BF)
    q_ref[...] = dot(block, wq_ref[...], 1, 0).astype(BF)
    third = D // GROUP
    t_ref[...] = block_ref[:, pl.ds(pl.multiple_of(step * third, 128), third)].T


def place_block(buffers, a, b, home, index, weight_kv, weight_q, split=False):
    tok = a.shape[0] * (2 if split else 1)
    shapes = ((D, 4 * tok), (4 * tok, 2 * GROUP * HEAD), (4 * tok, GROUP * HEAD))
    whole = pl.BlockSpec(a.shape, lambda h, place: (0, 0))
    anywhere = pl.BlockSpec(memory_space=pl.ANY)
    return pl.pallas_call(
        lambda *refs: place_kernel(split, *refs),
        grid_spec=pltpu.PrefetchScalarGridSpec(
            num_scalar_prefetch=1,
            grid=(GROUP,),
            in_specs=[
                whole, whole,
                pl.BlockSpec((D, 2 * HEAD), lambda h, place: (0, h)),
                pl.BlockSpec((D, HEAD), lambda h, place: (0, h)),
            ]
            + [anywhere] * len(buffers),
            out_specs=[
                pl.BlockSpec((D // GROUP, tok), lambda h, place: (h, place[0])),
                pl.BlockSpec((tok, 2 * HEAD), lambda h, place: (place[0], h)),
                pl.BlockSpec((tok, HEAD), lambda h, place: (place[0], h)),
            ],
            scratch_shapes=[pltpu.VMEM((tok, D), BF)],
        ),
        out_shape=[jax.ShapeDtypeStruct(shape, BF) for shape in shapes],
        input_output_aliases={5: 0, 6: 1, 7: 2} if buffers else {},
        compiler_params=pltpu.CompilerParams(vmem_limit_bytes=60 * 1024 * 1024),
        cost_estimate=pl.CostEstimate(
            flops=FIRST, bytes_accessed=8 * tok * D, transcendentals=0
        ),
    )(jnp.stack([index, home.astype(jnp.int32)]), a, b, weight_kv, weight_q, *buffers)


def finish_kernel(nz, place_ref, keep_ref, got_ref, low_ref, high_ref, near_ref, far_ref, *refs):
    outs, acc_ref = refs[:-1], refs[-1]
    first = place_ref[0] == 0

    @pl.when(first)
    def _():
        acc_ref[...] = dot(low_ref[...], far_ref[...], 1, 0)

    @pl.when(jnp.logical_not(first))
    def _():
        acc_ref[...] = dot(high_ref[...], near_ref[...], 1, 0)

    fine = acc_ref.shape[0] // nz
    for steps in range(nz):
        at = pl.multiple_of(lax.rem(place_ref[1] + steps, nz) * fine, 16)
        total = keep_ref[steps, 0].astype(F32) + got_ref[steps, 0].astype(F32)
        part = acc_ref[pl.ds(at, fine), :]
        for h in range(GROUP):
            cols = slice(3 * HEAD * h, 3 * HEAD * h + 2 * HEAD)
            rest = slice(3 * HEAD * h + 2 * HEAD, 3 * HEAD * (h + 1))
            added = total[:, cols] + part[:, 2 * HEAD * h : 2 * HEAD * (h + 1)]
            outs[steps][0, :, cols] = added.astype(BF)
            outs[steps][0, :, rest] = total[:, rest].astype(BF)


def finish(place, nz, keep, got, low, high, near, far):
    rows = D // 8
    shape = (4, rows // nz, COLS)
    both = pl.BlockSpec((nz, 1) + shape[1:], lambda n, place: (0, n, 0, 0))
    part = pl.BlockSpec((rows, low.shape[1]), lambda n, place: (n, 0))
    fixed = pl.BlockSpec(near.shape, lambda n, place: (0, 0))
    return pl.pallas_call(
        lambda *refs: finish_kernel(nz, *refs),
        grid_spec=pltpu.PrefetchScalarGridSpec(
            num_scalar_prefetch=1,
            grid=(4,),
            in_specs=[both, both, part, part, fixed, fixed],
            out_specs=[pl.BlockSpec((1,) + shape[1:], lambda n, place: (n, 0, 0))] * nz,
            scratch_shapes=[pltpu.VMEM((rows, near.shape[1]), F32)],
        ),
        out_shape=[jax.ShapeDtypeStruct(shape, BF)] * nz,
        compiler_params=pltpu.CompilerParams(vmem_limit_bytes=60 * 1024 * 1024),
        cost_estimate=pl.CostEstimate(
            flops=FIRST, bytes_accessed=12 * 1024 * 1024, transcendentals=0
        ),
    )(place, keep, got, low, high, near, far)


def input_kernel(place_ref, dkv_ref, extra_ref, dq_ref, wkv_ref, wq_ref, *refs):
    step = pl.program_id(0)
    late = place_ref[step] >= 2
    extra = jnp.where(late, extra_ref[...].astype(F32), 0.0)
    dkv = (dkv_ref[...].astype(F32) + extra).astype(BF)
    total = dot(dkv, wkv_ref[...], 1, 1) + dot(dq_ref[...], wq_ref[...], 1, 1)
    half = total.shape[0] // 2
    if len(refs) == 2:
        refs[0][...] = total[:half].astype(BF)
        refs[1][...] = total[half:].astype(BF)
        return
    top_ref, low_ref, left_ref, right_ref, own_ref = refs

    @pl.when(step == 0)
    def _():
        left_ref[:half, :] = (total[:half] + top_ref[...].astype(F32)).astype(BF)
        left_ref[half:, :] = total[half:].astype(BF)

    @pl.when(step == 1)
    def _():
        right_ref[:half, :] = total[:half].astype(BF)
        right_ref[half:, :] = (total[half:] + low_ref[...].astype(F32)).astype(BF)

    @pl.when(step == 2)
    def _():
        own_ref[...] = total.astype(BF)


def input_grads(blocks, dkv, extra, dq, weight_kv, weight_q, back=()):
    wide = dq.shape[1]
    tok = dq.shape[0] // 4
    rows = lambda cols: pl.BlockSpec((tok, cols), lambda n, place: (place[n], 0))
    whole = lambda rows, cols: pl.BlockSpec((rows, cols), lambda n, place: (0, 0))
    made = [(tok, D)] * 3 if back else [(tok // 2, D)] * 2
    return pl.pallas_call(
        input_kernel,
        grid_spec=pltpu.PrefetchScalarGridSpec(
            num_scalar_prefetch=1,
            grid=(len(blocks),),
            in_specs=[
                rows(2 * wide),
                pl.BlockSpec((tok, 2 * wide), lambda n, place: (jnp.maximum(place[n] - 2, 0), 0)),
                rows(wide), whole(D, 2 * wide), whole(D, wide),
            ]
            + [whole(tok // 2, D)] * len(back),
            out_specs=[whole(*shape) for shape in made],
        ),
        out_shape=[jax.ShapeDtypeStruct(shape, BF) for shape in made],
        compiler_params=pltpu.CompilerParams(vmem_limit_bytes=60 * 1024 * 1024),
        cost_estimate=pl.CostEstimate(
            flops=FIRST, bytes_accessed=12 * 1024 * 1024, transcendentals=0
        ),
    )(jnp.stack(blocks), dkv, extra, dq, weight_kv, weight_q, *back)


def add_kernel(*refs):
    total = refs[0][...].astype(F32)
    for ref in refs[1:-1]:
        total = total + ref[...].astype(F32)
    refs[-1][...] = total.astype(BF)


def add_up(parts, weight):
    return pl.pallas_call(
        add_kernel,
        out_shape=jax.ShapeDtypeStruct(parts[0].shape, BF),
        compiler_params=pltpu.CompilerParams(vmem_limit_bytes=60 * 1024 * 1024),
        cost_estimate=pl.CostEstimate(
            flops=512 * weight, bytes_accessed=weight, transcendentals=0
        ),
    )(*parts)


def block_of(array, index, size):
    return lax.dynamic_slice_in_dim(array, index * size, size, 0)


def put(array, part, index):
    return lax.dynamic_update_slice_in_dim(array, part, index * part.shape[0], 0)


def on_device(sizes, inputs, w_query, w_key, w_value, out_grad):
    c = lax.axis_index("c")
    y = lax.axis_index("y")
    z = lax.axis_index("z")
    xl = lax.axis_index("xl")
    nz, nh = sizes["z"], sizes["xh"]
    tok = inputs.shape[1]
    half = tok // 2
    home = xl == c

    def ring(value, axis, steps, count=4):
        return lax.ppermute(value, axis, [(i, (i + steps) % count) for i in range(count)])

    def side_ring(value, axis, steps, count, own):
        pairs = []
        for side in range(2):
            core = side if own else 1 - side
            for i in range(count):
                j = (i + steps) % count
                pairs.append(((side * count + i) * 2 + core, (side * count + j) * 2 + core))
        return lax.ppermute(value, ("xl", axis, "c"), pairs)

    def swap_sides(value):
        return lax.ppermute(value, ("xl", "c"), [(1, 2), (2, 1)])

    at = lambda steps: (y + steps) % 4
    wide = GROUP * HEAD

    def crossed(value, steps):
        pairs = []
        for side in range(2):
            for i in range(4):
                for core in range(2):
                    there = ((core * 4 + (i + steps) % 4) * 2) + side
                    if steps or side != core:
                        pairs.append(((side * 4 + i) * 2 + core, there))
        return lax.ppermute(value, ("xl", "y", "c"), pairs)

    own = inputs[0]
    moved = swap_sides(own)
    left_home = side_ring(own, "y", 1, 4, True)
    right_home = side_ring(own, "y", -1, 4, True)
    weight_q, weight_kv = pick_weights(y, w_query, w_key, w_value)
    moved, left_home, right_home, weight_q, weight_kv, out_grad = lax.optimization_barrier(
        (moved, left_home, right_home, weight_q, weight_kv, out_grad)
    )
    left_away = side_ring(moved, "y", 1, 4, False)
    right_away = side_ring(moved, "y", -1, 4, False)
    cols = lambda index: lax.dynamic_slice_in_dim(out_grad[0], index * wide, wide, 1)
    dout_own = cols(y)
    dout_own = jnp.where(home, dout_own, crossed(dout_own, 0))
    dout_left = crossed(cols(at(1)), 1)
    dout_right = crossed(cols(at(-1)), -1)
    dout_far = crossed(cols(at(2)), 2)
    buffers = place_block((), own, moved, home, y, weight_kv, weight_q)
    dout_all = jnp.zeros((4 * tok, wide), BF)
    for part, index in ((dout_own, y), (dout_left, at(-1)), (dout_right, at(1)), (dout_far, at(2))):
        dout_all = put(dout_all, part, index)
    buffers, dout_all, left_away, right_away = lax.optimization_barrier(
        (buffers, dout_all, left_away, right_away)
    )
    far_top = jnp.where(home, left_home[:half], left_away[:half])
    far_low = jnp.where(home, right_home[half:], right_away[half:])
    far_top, far_low = lax.optimization_barrier((far_top, far_low))
    far_top = ring(far_top, "y", 1)
    far_low = ring(far_low, "y", -1)
    buffers = place_block(buffers, left_home, left_away, home, at(-1), weight_kv, weight_q)
    buffers = place_block(buffers, right_home, right_away, home, at(1), weight_kv, weight_q)
    tokens, kv, q = place_block(
        buffers, far_top, far_low, home, at(2), weight_kv, weight_q, split=True
    )

    halo = lax.ppermute(kv[2 * tok :], "c", [(0, 1)])
    bias = jnp.where(c == 0, -1e30, 0.0).astype(F32).reshape(1, 1)
    mine = jnp.stack([c, z])
    dq, dkv, dhalo, give, keep, low, high = attention(
        mine, bias, q, kv, halo, dout_all, tokens, nz
    )
    far_dhalo = lax.ppermute(dhalo, "c", [(1, 0)])
    got = lax.ppermute(give, "c", [(0, 1), (1, 0)])
    high = lax.ppermute(high, "c", [(0, 1)])
    far_parts = input_grads([at(2)], dkv, far_dhalo, dq, weight_kv, weight_q)
    back_top = ring(far_parts[0], "y", -1)
    back_low = ring(far_parts[1], "y", 1)
    keep, far_parts = lax.optimization_barrier((keep, far_parts))
    slabs = list(finish(mine, nz, keep, got, low, high, dhalo, far_dhalo))
    sent = [ring(slabs[steps], "z", steps, nz) for steps in range(1, nz)]
    dkv, slabs[0] = lax.optimization_barrier((dkv, slabs[0]))
    part_left, part_right, part_own = input_grads(
        [at(-1), at(1), y], dkv, far_dhalo, dq, weight_kv, weight_q, (back_top, back_low)
    )
    from_right = ring(part_left, "y", -1)
    from_left = ring(part_right, "y", 1)
    *sent, part_own = lax.optimization_barrier((*sent, part_own))
    share = add_up([slabs[0]] + sent, 4 * 1024 * 1024 * 1024)

    around = 2 * nh
    arrived = []
    for steps in range(1, around):
        pairs = []
        for core in range(2):
            for xh in range(nh):
                source = (xh * 2 + core + steps) % around
                pairs.append(
                    (((source % 2) * nh + source // 2) * 2 + core, (core * nh + xh) * 2 + core)
                )
        arrived.append(lax.ppermute(share, ("xl", "xh", "c"), pairs))
    *arrived, from_left, from_right = lax.optimization_barrier((*arrived, from_left, from_right))
    summed = share.astype(F32)
    for part in arrived:
        summed = summed + part.astype(F32)
    summed = summed.astype(BF)
    input_grad = part_own.astype(F32) + from_right.astype(F32) + from_left.astype(F32)
    input_grad = input_grad.astype(BF)
    away_grad = swap_sides(input_grad)

    fine = D // 8 // nz
    piece = lambda index: lax.dynamic_index_in_dim(summed, index % 4, 0, keepdims=False)
    gathered = jnp.zeros((3, fine, D), BF)

    def spread(gathered, piece, index):
        column = lambda i: piece[:, i * HEAD : (i + 1) * HEAD]
        parts = [[column(3 * h + part) for h in range(GROUP)] for part in (2, 0, 1)]
        parts = jnp.stack([jnp.concatenate(part, axis=1) for part in parts])
        return lax.dynamic_update_slice_in_dim(gathered, parts, index * wide, 2)

    gathered = spread(gathered, piece(y), y)
    for steps in range(1, 4):
        gathered = spread(gathered, side_ring(piece(y + steps), "y", steps, 4, True), at(-steps))
    result = jnp.zeros((3, nz * fine, D), BF)
    result = lax.dynamic_update_slice_in_dim(result, gathered, z * fine, 1)
    for steps in range(1, nz):
        result = lax.dynamic_update_slice_in_dim(
            result, side_ring(gathered, "z", steps, nz, True), (z - steps) % nz * fine, 1
        )
    result, away_grad = lax.optimization_barrier((result, away_grad))
    other = lax.ppermute(result, ("xl", "c"), [(0, 1), (3, 2)])
    input_grad = jnp.where(home, input_grad, away_grad)
    outs = [jnp.where(home, result[part], other[part]).astype(F32) for part in range(3)]
    return input_grad[None], outs[0], outs[1], outs[2]


def solution(mesh):
    dp = mesh.shape["dp"]
    nz = 4 if dp == 16 else 1
    nh = dp // 2 // nz
    sizes = {"xl": 2, "y": 4, "xh": nh, "z": nz, "c": 2}
    fine = Mesh(mesh.devices.reshape(tuple(sizes.values())), tuple(sizes))
    block, rollouts = ("xl", "y"), ("xh", "z", "c")
    placed = (P(rollouts, block, None), P(), P(), P(), P(rollouts, block, None))
    return jax.shard_map(
        lambda *arrays: on_device(sizes, *arrays),
        mesh=fine,
        in_specs=placed,
        out_specs=(P(rollouts, block, None), P(block, None), P(block, None), P(block, None)),
        check_vma=False,
    )
```

profile of v0, /device:TPU:1, one launch (start us, length us, event | category | flops | bytes accessed | tf_op | source)
XLA Modules:
  0.0 232.3 jit_solution(9214505985885568085)
XLA Ops:
  0.6 4.5 %collective-permute-start = (bf16[384,1536]{1,0:T(8,128)(2,1)}, bf16[384,1536]{1,0:T(8,128)(2,1)}, u32[]{:S(2)}, u32[]{:S(2)}) collective-permute-start(bf16[384,1536]{1,0:T(8,128)(2,1)} %bitcast.68), channel_id=1, source_target_pairs={{1,64},{64,1},{3,66},{66,3},{5,68},{68,5},{7,70},{70,7},{9,72},{72... | collective-permute-start | bytes 3538952 | tf_op jit(solution)/shard_map/ppermute | solution.py:380
  5.2 1.7 collective-permute-start.1
  6.8 1.8 collective-permute-start.2
  8.6 4.9 %shard_map.84 = (bf16[1536,384]{1,0:T(8,128)(2,1)}, bf16[1536,768]{1,0:T(8,128)(2,1)}) custom-call(s32[1]{0:T(128)} %bitcast.6.place_ref, bf16[1536,1536]{1,0:T(8,128)(2,1)} %query_ref.1, bf16[1536,1536]{1,0:T(8,128)(2,1)} %key_ref.1, bf16[1536,1536]{1,0:T(8,128)(2,1)} %value_ref.1), custom_call_target="tpu_custom_call" | custom-call | flops 1099511627776 | bytes 7077888 | tf_op jit(solution)/shard_map/pallas_call | solution.py:150
  15.5 4.1 %collective-permute-done.refs_2_ = bf16[384,1536]{1,0:T(8,128)(2,1)} collective-permute-done((bf16[384,1536]{1,0:T(8,128)(2,1)}, bf16[384,1536]{1,0:T(8,128)(2,1)}, u32[]{:S(2)}, u32[]{:S(2)}) %collective-permute-start) | collective-permute-done | bytes 1179680 | tf_op jit(solution)/shard_map/ppermute | solution.py:380
  19.6 3.2 %collective-permute-start.7 = (bf16[384,1536]{1,0:T(8,128)(2,1)}, bf16[384,1536]{1,0:T(8,128)(2,1)}, u32[]{:S(2)}, u32[]{:S(2)}) collective-permute-start(bf16[384,1536]{1,0:T(8,128)(2,1)} %collective-permute-done.refs_2_), channel_id=1, source_target_pairs={{1,17},{17,33},{33,49},{49,1},{64,80},{80,96},{96,112},{112,64},{3... | collective-permute-start | bytes 3538952 | tf_op jit(solution)/shard_map/ppermute | solution.py:377
  22.8 3.4 %collective-permute-start.8 = (bf16[384,1536]{1,0:T(8,128)(2,1)}, bf16[384,1536]{1,0:T(8,128)(2,1)}, u32[]{:S(2)}, u32[]{:S(2)}) collective-permute-start(bf16[384,1536]{1,0:T(8,128)(2,1)} %collective-permute-done.refs_2_), channel_id=1, source_target_pairs={{1,49},{17,1},{33,17},{49,33},{64,112},{80,64},{96,80},{112,96},{3... | collective-permute-start | bytes 3538952 | tf_op jit(solution)/shard_map/ppermute | solution.py:377
  26.2 1.1 dynamic-slice_bitcast_fusion
  27.3 3.8 %collective-permute-start.3 = (bf16[384,384]{1,0:T(8,128)(2,1)}, bf16[384,384]{1,0:T(8,128)(2,1)}, u32[]{:S(2)}, u32[]{:S(2)}) collective-permute-start(bf16[384,384]{1,0:T(8,128)(2,1)} %get-tuple-element.126), channel_id=1, source_target_pairs={{1,64},{17,80},{33,96},{49,112},{64,1},{80,17},{96,33},{112,49},{3... | collective-permute-start | bytes 884744 | tf_op jit(solution)/shard_map/ppermute | solution.py:393
  31.2 3.8 %collective-permute-start.5 = (bf16[384,384]{1,0:T(8,128)(2,1)}, bf16[384,384]{1,0:T(8,128)(2,1)}, u32[]{:S(2)}, u32[]{:S(2)}) collective-permute-start(bf16[384,384]{1,0:T(8,128)(2,1)} %get-tuple-element.124), channel_id=1, source_target_pairs={{0,48},{1,112},{16,0},{17,64},{32,16},{33,80},{48,32},{49,96},{64,... | collective-permute-start | bytes 884744 | tf_op jit(solution)/shard_map/ppermute | solution.py:393
  35.1 6.8 %shard_map.85 = (bf16[1536,1536]{1,0:T(8,128)(2,1)}, bf16[1536,768]{1,0:T(8,128)(2,1)}, bf16[1536,384]{1,0:T(8,128)(2,1)}) custom-call(s32[2]{0:T(128)} %get-tuple-element.167.refs_0_, bf16[384,1536]{1,0:T(8,128)(2,1)} %bitcast.71, bf16[384,1536]{1,0:T(8,128)(2,1)} %collective-permute-done.refs_2_, bf16[1536,768]{1,0:T(8,128)(2,1)} %get-tuple-element.66.refs_3_.wkv_ref, ...), custom_call_target="tpu_custom_call" | custom-call | flops 1099511627776 | bytes 4718592 | tf_op jit(solution)/shard_map/pallas_call | solution.py:201
  42.3 1.2 select_dynamic-update-slice_fusion
  45.5 5.1 %collective-permute-done.6 = bf16[384,384]{1,0:T(8,128)(2,1)S(1)} collective-permute-done((bf16[384,384]{1,0:T(8,128)(2,1)S(1)}, bf16[384,384]{1,0:T(8,128)(2,1)S(1)}, u32[]{:S(2)}, u32[]{:S(2)}) %collective-permute-start.6) | collective-permute-done | bytes 294944 | tf_op jit(solution)/shard_map/ppermute | solution.py:393
  50.7 1.7 collective-permute-done.8.refs_2_
  52.3 2.1 slice_select_fusion.3
  54.5 2.1 slice_select_fusion.4
  56.6 3.1 %collective-permute-start.10 = (bf16[192,1536]{1,0:T(8,128)(2,1)}, bf16[192,1536]{1,0:T(8,128)(2,1)}, u32[]{:S(2)}, u32[]{:S(2)}) collective-permute-start(bf16[192,1536]{1,0:T(8,128)(2,1)} %slice_select_fusion.3), channel_id=1, source_target_pairs={{0,48},{16,0},{32,16},{48,32},{1,49},{17,1},{33,17},{49,33},{2,50}... | collective-permute-start | bytes 1769480 | tf_op jit(solution)/shard_map/ppermute | solution.py:368
  59.7 6.8 %shard_map.86 = (bf16[1536,1536]{1,0:T(8,128)(2,1)}, bf16[1536,768]{1,0:T(8,128)(2,1)}, bf16[1536,384]{1,0:T(8,128)(2,1)}) custom-call(s32[2]{0:T(128)} %pad_add_fusion.4.refs_0_, bf16[384,1536]{1,0:T(8,128)(2,1)} %collective-permute-done.1.refs_1_, ...), custom_call_target="tpu_custom_call", output_to_operand_aliasing={{0}: (5, {}), {1}: (6, {}), {2}: (7, {})} | custom-call | flops 1099511627776 | bytes 4718592 | tf_op jit(solution)/shard_map/pallas_call | solution.py:201
  66.4 6.7 %shard_map.87 = (bf16[1536,1536]{1,0:T(8,128)(2,1)}, bf16[1536,768]{1,0:T(8,128)(2,1)}, bf16[1536,384]{1,0:T(8,128)(2,1)}) custom-call(s32[2]{0:T(128)} %get-tuple-element.168.refs_0_, bf16[384,1536]{1,0:T(8,128)(2,1)} %collective-permute-done.2.refs_1_, ...), custom_call_target="tpu_custom_call", output_to_operand_aliasing={{0}: (5, {}), {1}: (6, {}), {2}: (7, {})} | custom-call | flops 1099511627776 | bytes 4718592 | tf_op jit(solution)/shard_map/pallas_call | solution.py:201
  73.1 1.8 collective-permute-done.9.refs_1_
  74.9 6.2 %shard_map.88 = (bf16[1536,1536]{1,0:T(8,128)(2,1)}, bf16[1536,768]{1,0:T(8,128)(2,1)}, bf16[1536,384]{1,0:T(8,128)(2,1)}) custom-call(s32[2]{0:T(128)} %pad_add_fusion.1.refs_0_, bf16[192,1536]{1,0:T(8,128)(2,1)} %collective-permute-done.9.refs_1_, ...), custom_call_target="tpu_custom_call", output_to_operand_aliasing={{0}: (5, {}), {1}: (6, {}), {2}: (7, {})} | custom-call | flops 1099511627776 | bytes 4718592 | tf_op jit(solution)/shard_map/pallas_call | solution.py:201
  81.1 1.3 slice.145
  82.4 1.5 collective-permute-start.11
  84.5 3.6 %collective-permute-done.11.refs_4_ = bf16[768,768]{1,0:T(8,128)(2,1)S(1)} collective-permute-done((bf16[768,768]{1,0:T(8,128)(2,1)S(1)}, bf16[768,768]{1,0:T(8,128)(2,1)S(1)}, u32[]{:S(2)}, u32[]{:S(2)}) %collective-permute-start.11) | collective-permute-done | bytes 1179680 | tf_op jit(solution)/shard_map/ppermute | solution.py:429
  89.2 34.5 %shard_map.89 = (bf16[1536,384]{1,0:T(8,128)(2,1)}, bf16[1536,768]{1,0:T(8,128)(2,1)}, bf16[768,768]{1,0:T(8,128)(2,1)}, bf16[4,4,48,1152]{3,2,1,0:T(8,128)(2,1)...) custom-call(s32[2]{0:T(128)} %pad_add_fusion.refs_0_, ...), custom_call_target="tpu_custom_call" | custom-call | flops 19025362944 | bytes 28311552 | tf_op jit(solution)/shard_map/pallas_call | solution.py:112
  123.7 2.1 collective-permute-start.12
  126.4 1.3 collective-permute-start.14
  129.4 5.1 %shard_map.90 = (bf16[192,1536]{1,0:T(8,128)(2,1)}, bf16[192,1536]{1,0:T(8,128)(2,1)}) custom-call(s32[1]{0:T(128)} %bitcast.3.place_ref, bf16[1536,768]{1,0:T(8,128)(2,1)} %get-tuple-element.104.dkv_ref, bf16[768,768]{1,0:T(8,128)(2,1)} %copy-done.4, bf16[1536,384]{1,0:T(8,128)(2,1)} %get-tuple-element.93.dq_ref, ...), custom_call_target="tpu_custom_call" | custom-call | flops 1099511627776 | bytes 12582912 | tf_op jit(solution)/shard_map/pallas_call | solution.py:310
  134.5 1.4 collective-permute-start.19
  136.0 6.7 %shard_map.91 = (bf16[4,48,1152]{2,1,0:T(8,128)(2,1)}, bf16[4,48,1152]{2,1,0:T(8,128)(2,1)}, bf16[4,48,1152]{2,1,0:T(8,128)(2,1)}, bf16[4,48,1152]{2,1,0:T(8,128)(2,1)}) custom-call(s32[2]{0:T(128)} %pad_add_fusion.refs_0_, bf16[4,4,48,1152]{3,2,1,0:T(8,128)(2,1)} %get-tuple-element.96.refs_1_, bf16[4,4,48,1152]{3,2,1,0:T(8,128)(2,1)} %collective-permute-done.13.refs_2_, ...), custom_call_target="tpu_custom_call" | custom-call | flops 1099511627776 | bytes 12582912 | tf_op jit(solution)/shard_map/pallas_call | solution.py:259
  142.7 1.7 collective-permute-start.15
  144.3 3.3 %collective-permute-start.16 = (bf16[4,48,1152]{2,1,0:T(8,128)(2,1)}, bf16[4,48,1152]{2,1,0:T(8,128)(2,1)}, u32[]{:S(2)}, u32[]{:S(2)}) collective-permute-start(bf16[4,48,1152]{2,1,0:T(8,128)(2,1)} %get-tuple-element.101), channel_id=1, source_target_pairs={{0,4},{2,6},{4,0},{6,2},{1,5},{3,7},{5,1},{7,3},{8,12},{10,14},{12... | collective-permute-start | bytes 1327112 | tf_op jit(solution)/shard_map/ppermute | solution.py:368
  149.1 11.0 %shard_map.92 = (bf16[384,1536]{1,0:T(8,128)(2,1)}, bf16[384,1536]{1,0:T(8,128)(2,1)}, bf16[384,1536]{1,0:T(8,128)(2,1)}) custom-call(s32[3]{0:T(128)} %pad_add_fusion.5.place_ref, bf16[1536,768]{1,0:T(8,128)(2,1)} %get-tuple-element.104.dkv_ref, bf16[768,768]{1,0:T(8,128)(2,1)} %copy-done.4, bf16[1536,384]{1,0:T(8,128)(2,1)} %get-tuple-element.93.dq_ref, ...), custom_call_target="tpu_custom_call" | custom-call | flops 1099511627776 | bytes 12582912 | tf_op jit(solution)/shard_map/pallas_call | solution.py:310
  160.3 2.5 %collective-permute-start.24 = (bf16[384,1536]{1,0:T(8,128)(2,1)}, bf16[384,1536]{1,0:T(8,128)(2,1)}, u32[]{:S(2)}, u32[]{:S(2)}) collective-permute-start(bf16[384,1536]{1,0:T(8,128)(2,1)} %get-tuple-element.112), channel_id=1, source_target_pairs={{0,48},{16,0},{32,16},{48,32},{1,49},{17,1},{33,17},{49,33},{2,50}... | collective-permute-start | bytes 3538952 | tf_op jit(solution)/shard_map/ppermute | solution.py:368
  162.8 2.8 %collective-permute-done.16.refs_2_ = bf16[4,48,1152]{2,1,0:T(8,128)(2,1)} collective-permute-done((bf16[4,48,1152]{2,1,0:T(8,128)(2,1)}, bf16[4,48,1152]{2,1,0:T(8,128)(2,1)}, u32[]{:S(2)}, u32[]{:S(2)}) %collective-permute-start.16) | collective-permute-done | bytes 442400 | tf_op jit(solution)/shard_map/ppermute | solution.py:368
  166.5 2.4 %shard_map.93 = bf16[4,48,1152]{2,1,0:T(8,128)(2,1)} custom-call(bf16[4,48,1152]{2,1,0:T(8,128)(2,1)} %get-tuple-element.107.refs_0_, bf16[4,48,1152]{2,1,0:T(8,128)(2,1)} %collective-permute-done.15.refs_1_, bf16[4,48,1152]{2,1,0:T(8,128)(2,1)} %collective-permute-done.16.refs_2_, bf16[4,48,1152]{2,1,0:T(8,128)(2,1)} %collective-permute-done.17.refs_3_), custom_call_target="tpu_custom_call" | custom-call | flops 2199023255552 | bytes 4294967296 | tf_op jit(solution)/shard_map/pallas_call | solution.py:339
  168.9 4.3 %collective-permute-start.20 = (bf16[4,48,1152]{2,1,0:T(8,128)(2,1)}, bf16[4,48,1152]{2,1,0:T(8,128)(2,1)S(1)}, u32[]{:S(2)}, u32[]{:S(2)}) collective-permute-start(bf16[4,48,1152]{2,1,0:T(8,128)(2,1)} %shard_map.93), channel_id=1, source_target_pairs={{64,0},{72,8},{9,65},{1,73},{66,2},{74,10},{11,67},{3,75},{68,4},{... | collective-permute-start | bytes 1327112 | tf_op jit(solution)/shard_map/ppermute | solution.py:463
  174.0 3.1 %collective-permute-start.22 = (bf16[4,48,1152]{2,1,0:T(8,128)(2,1)}, bf16[4,48,1152]{2,1,0:T(8,128)(2,1)S(1)}, u32[]{:S(2)}, u32[]{:S(2)}) collective-permute-start(bf16[4,48,1152]{2,1,0:T(8,128)(2,1)} %shard_map.93), channel_id=1, source_target_pairs={{72,0},{64,8},{1,65},{9,73},{74,2},{66,10},{3,67},{11,75},{76,4},{... | collective-permute-start | bytes 1327112 | tf_op jit(solution)/shard_map/ppermute | solution.py:463
  177.1 4.6 %collective-permute-done.20 = bf16[4,48,1152]{2,1,0:T(8,128)(2,1)S(1)} collective-permute-done((bf16[4,48,1152]{2,1,0:T(8,128)(2,1)}, bf16[4,48,1152]{2,1,0:T(8,128)(2,1)S(1)}, u32[]{:S(2)}, u32[]{:S(2)}) %collective-permute-start.20) | collective-permute-done | bytes 442400 | tf_op jit(solution)/shard_map/ppermute | solution.py:463
  181.8 5.2 %collective-permute-done.22 = bf16[4,48,1152]{2,1,0:T(8,128)(2,1)S(1)} collective-permute-done((bf16[4,48,1152]{2,1,0:T(8,128)(2,1)}, bf16[4,48,1152]{2,1,0:T(8,128)(2,1)S(1)}, u32[]{:S(2)}, u32[]{:S(2)}) %collective-permute-start.22) | collective-permute-done | bytes 442400 | tf_op jit(solution)/shard_map/ppermute | solution.py:463
  187.0 1.2 add_convert_fusion.1
  190.4 2.1 add_convert_fusion
  192.5 7.0 %collective-permute-start.31 = (bf16[384,1536]{1,0:T(8,128)(2,1)S(1)}, bf16[384,1536]{1,0:T(8,128)(2,1)S(1)}, u32[]{:S(2)}, u32[]{:S(2)}) collective-permute-start(bf16[384,1536]{1,0:T(8,128)(2,1)S(1)} %add_convert_fusion), channel_id=1, source_target_pairs={{1,64},{64,1},{3,66},{66,3},{5,68},{68,5},{7,70},{70,7},{9,72},{72... | collective-permute-start | bytes 3538952 | tf_op jit(solution)/shard_map/ppermute | solution.py:380
  202.4 11.2 %collective-permute-done.31 = bf16[384,1536]{1,0:T(8,128)(2,1)S(1)} collective-permute-done((bf16[384,1536]{1,0:T(8,128)(2,1)S(1)}, bf16[384,1536]{1,0:T(8,128)(2,1)S(1)}, u32[]{:S(2)}, u32[]{:S(2)}) %collective-permute-start.31) | collective-permute-done | bytes 1179680 | tf_op jit(solution)/shard_map/ppermute | solution.py:380
  213.6 1.3 collective-permute-start.32
  214.9 1.1 select_bitcast_fusion
  216.0 14.4 %collective-permute-done.32 = bf16[3,192,1536]{2,1,0:T(8,128)(2,1)S(1)} collective-permute-done((bf16[3,192,1536]{2,1,0:T(8,128)(2,1)S(1)}, bf16[3,192,1536]{2,1,0:T(8,128)(2,1)S(1)}, u32[]{:S(2)}, u32[]{:S(2)}) %collective-permute-start.32) | collective-permute-done | bytes 1769504 | tf_op jit(solution)/shard_map/ppermute | solution.py:493
  230.4 1.9 fusion.1
  (85 shorter events, 16.6 us)
Async XLA Ops:
  0.6 19.0 %collective-permute-start = (bf16[384,1536]{1,0:T(8,128)(2,1)}, bf16[384,1536]{1,0:T(8,128)(2,1)}, u32[]{:S(2)}, u32[]{:S(2)}) collective-permute-start(bf16[384,1536]{1,0:T(8,128)(2,1)} %bitcast.68), channel_id=1, source_target_pairs={{1,64},{64,1},{3,66},{66,3},{5,68},{68,5},{7,70},{70,7},{9,72},{72... | collective-permute-start | bytes 3538952 | tf_op jit(solution)/shard_map/ppermute | solution.py:380
  5.2 14.5 %collective-permute-start.1 = (bf16[384,1536]{1,0:T(8,128)(2,1)}, bf16[384,1536]{1,0:T(8,128)(2,1)}, u32[]{:S(2)}, u32[]{:S(2)}) collective-permute-start(bf16[384,1536]{1,0:T(8,128)(2,1)} %bitcast.69), channel_id=1, source_target_pairs={{0,16},{16,32},{32,48},{48,0},{65,81},{81,97},{97,113},{113,65},{2... | collective-permute-start | bytes 3538952 | tf_op jit(solution)/shard_map/ppermute | solution.py:377
  6.8 12.8 %collective-permute-start.2 = (bf16[384,1536]{1,0:T(8,128)(2,1)}, bf16[384,1536]{1,0:T(8,128)(2,1)}, u32[]{:S(2)}, u32[]{:S(2)}) collective-permute-start(bf16[384,1536]{1,0:T(8,128)(2,1)} %bitcast.70), channel_id=1, source_target_pairs={{0,48},{16,0},{32,16},{48,32},{65,113},{81,65},{97,81},{113,97},{2... | collective-permute-start | bytes 3538952 | tf_op jit(solution)/shard_map/ppermute | solution.py:377
  8.6 17.6 %copy-start = (bf16[1,384,1536]{2,1,0:T(8,128)(2,1)S(1)}, bf16[1,384,1536]{2,1,0:T(8,128)(2,1)}, u32[]{:S(2)}) copy-start(bf16[1,384,1536]{2,1,0:T(8,128)(2,1)} %param.9) | copy-start | bytes 3538948
  19.6 31.0 %collective-permute-start.7 = (bf16[384,1536]{1,0:T(8,128)(2,1)}, bf16[384,1536]{1,0:T(8,128)(2,1)}, u32[]{:S(2)}, u32[]{:S(2)}) collective-permute-start(bf16[384,1536]{1,0:T(8,128)(2,1)} %collective-permute-done.refs_2_), channel_id=1, source_target_pairs={{1,17},{17,33},{33,49},{49,1},{64,80},{80,96},{96,112},{112,64},{3... | collective-permute-start | bytes 3538952 | tf_op jit(solution)/shard_map/ppermute | solution.py:377
  22.8 29.5 %collective-permute-start.8 = (bf16[384,1536]{1,0:T(8,128)(2,1)}, bf16[384,1536]{1,0:T(8,128)(2,1)}, u32[]{:S(2)}, u32[]{:S(2)}) collective-permute-start(bf16[384,1536]{1,0:T(8,128)(2,1)} %collective-permute-done.refs_2_), channel_id=1, source_target_pairs={{1,49},{17,1},{33,17},{49,33},{64,112},{80,64},{96,80},{112,96},{3... | collective-permute-start | bytes 3538952 | tf_op jit(solution)/shard_map/ppermute | solution.py:377
  27.3 14.5 %collective-permute-start.3 = (bf16[384,384]{1,0:T(8,128)(2,1)}, bf16[384,384]{1,0:T(8,128)(2,1)}, u32[]{:S(2)}, u32[]{:S(2)}) collective-permute-start(bf16[384,384]{1,0:T(8,128)(2,1)} %get-tuple-element.126), channel_id=1, source_target_pairs={{1,64},{17,80},{33,96},{49,112},{64,1},{80,17},{96,33},{112,49},{3... | collective-permute-start | bytes 884744 | tf_op jit(solution)/shard_map/ppermute | solution.py:393
  31.1 12.3 %collective-permute-start.4 = (bf16[384,384]{1,0:T(8,128)(2,1)}, bf16[384,384]{1,0:T(8,128)(2,1)}, u32[]{:S(2)}, u32[]{:S(2)}) collective-permute-start(bf16[384,384]{1,0:T(8,128)(2,1)} %get-tuple-element.125), channel_id=1, source_target_pairs={{0,16},{1,80},{16,32},{17,96},{32,48},{33,112},{48,0},{49,64},{64,... | collective-permute-start | bytes 884744 | tf_op jit(solution)/shard_map/ppermute | solution.py:393
  31.2 13.3 %collective-permute-start.5 = (bf16[384,384]{1,0:T(8,128)(2,1)}, bf16[384,384]{1,0:T(8,128)(2,1)}, u32[]{:S(2)}, u32[]{:S(2)}) collective-permute-start(bf16[384,384]{1,0:T(8,128)(2,1)} %get-tuple-element.124), channel_id=1, source_target_pairs={{0,48},{1,112},{16,0},{17,64},{32,16},{33,80},{48,32},{49,96},{64,... | collective-permute-start | bytes 884744 | tf_op jit(solution)/shard_map/ppermute | solution.py:393
  35.1 6.8 %copy-start.3 = (bf16[384,384]{1,0:T(8,128)(2,1)S(1)}, bf16[384,384]{1,0:T(8,128)(2,1)}, u32[]{:S(2)}) copy-start(bf16[384,384]{1,0:T(8,128)(2,1)} %get-tuple-element.123) | copy-start | bytes 884740
  41.9 8.7 %collective-permute-start.6 = (bf16[384,384]{1,0:T(8,128)(2,1)S(1)}, bf16[384,384]{1,0:T(8,128)(2,1)S(1)}, u32[]{:S(2)}, u32[]{:S(2)}) collective-permute-start(bf16[384,384]{1,0:T(8,128)(2,1)S(1)} %copy-done.3), channel_id=1, source_target_pairs={{0,32},{1,96},{16,48},{17,112},{32,0},{33,64},{48,16},{49,80},{64,... | collective-permute-start | bytes 884744 | tf_op jit(solution)/shard_map/ppermute | solution.py:393
  50.6 5.9 %copy-start.1 = (bf16[1536,384]{1,0:T(8,128)(2,1)}, bf16[1536,384]{1,0:T(8,128)(2,1)S(1)}, u32[]{:S(2)}) copy-start(bf16[1536,384]{1,0:T(8,128)(2,1)S(1)} %constant_dynamic-update-slice_fusion.4.refs_5_) | copy-start | bytes 3538948
  56.6 16.5 %collective-permute-start.10 = (bf16[192,1536]{1,0:T(8,128)(2,1)}, bf16[192,1536]{1,0:T(8,128)(2,1)}, u32[]{:S(2)}, u32[]{:S(2)}) collective-permute-start(bf16[192,1536]{1,0:T(8,128)(2,1)} %slice_select_fusion.3), channel_id=1, source_target_pairs={{0,48},{16,0},{32,16},{48,32},{1,49},{17,1},{33,17},{49,33},{2,50}... | collective-permute-start | bytes 1769480 | tf_op jit(solution)/shard_map/ppermute | solution.py:368
  59.7 15.2 %collective-permute-start.9 = (bf16[192,1536]{1,0:T(8,128)(2,1)}, bf16[192,1536]{1,0:T(8,128)(2,1)}, u32[]{:S(2)}, u32[]{:S(2)}) collective-permute-start(bf16[192,1536]{1,0:T(8,128)(2,1)} %slice_select_fusion.4), channel_id=1, source_target_pairs={{0,16},{16,32},{32,48},{48,0},{1,17},{17,33},{33,49},{49,1},{2,18}... | collective-permute-start | bytes 1769480 | tf_op jit(solution)/shard_map/ppermute | solution.py:368
  82.4 5.7 %collective-permute-start.11 = (bf16[768,768]{1,0:T(8,128)(2,1)S(1)}, bf16[768,768]{1,0:T(8,128)(2,1)S(1)}, u32[]{:S(2)}, u32[]{:S(2)}) collective-permute-start(bf16[768,768]{1,0:T(8,128)(2,1)S(1)} %slice.145), channel_id=1, source_target_pairs={{0,1},{2,3},{4,5},{6,7},{8,9},{10,11},{12,13},{14,15},{16,17},{18,... | collective-permute-start | bytes 3538952 | tf_op jit(solution)/shard_map/ppermute | solution.py:429
  88.1 1.0 copy-start.5
  123.7 4.7 %collective-permute-start.12 = (bf16[768,768]{1,0:T(8,128)(2,1)}, bf16[768,768]{1,0:T(8,128)(2,1)S(1)}, u32[]{:S(2)}, u32[]{:S(2)}) collective-permute-start(bf16[768,768]{1,0:T(8,128)(2,1)} %get-tuple-element.92.refs_5_), channel_id=1, source_target_pairs={{1,0},{3,2},{5,4},{7,6},{9,8},{11,10},{13,12},{15,14},{17,16},{19,... | collective-permute-start | bytes 3538952 | tf_op jit(solution)/shard_map/ppermute | solution.py:435
  126.4 9.6 %collective-permute-start.13 = (bf16[4,4,48,1152]{3,2,1,0:T(8,128)(2,1)}, bf16[4,4,48,1152]{3,2,1,0:T(8,128)(2,1)}, u32[]{:S(2)}, u32[]{:S(2)}) collective-permute-start(bf16[4,4,48,1152]{3,2,1,0:T(8,128)(2,1)} %get-tuple-element.97), channel_id=1, source_target_pairs={{0,1},{1,0},{2,3},{3,2},{4,5},{5,4},{6,7},{7,6},{8,9},{9,8},{10,11... | collective-permute-start | bytes 5308424 | tf_op jit(solution)/shard_map/ppermute | solution.py:436
  126.4 9.6 %collective-permute-start.14 = (bf16[768,768]{1,0:T(8,128)(2,1)}, bf16[768,768]{1,0:T(8,128)(2,1)}, u32[]{:S(2)}, u32[]{:S(2)}) collective-permute-start(bf16[768,768]{1,0:T(8,128)(2,1)} %get-tuple-element.99), channel_id=1, source_target_pairs={{0,1},{2,3},{4,5},{6,7},{8,9},{10,11},{12,13},{14,15},{16,17},{18,... | collective-permute-start | bytes 3538952 | tf_op jit(solution)/shard_map/ppermute | solution.py:437
  128.4 1.0 copy-start.4
  134.5 13.9 %collective-permute-start.18 = (bf16[192,1536]{1,0:T(8,128)(2,1)}, bf16[192,1536]{1,0:T(8,128)(2,1)}, u32[]{:S(2)}, u32[]{:S(2)}) collective-permute-start(bf16[192,1536]{1,0:T(8,128)(2,1)} %get-tuple-element.94), channel_id=1, source_target_pairs={{0,48},{16,0},{32,16},{48,32},{1,49},{17,1},{33,17},{49,33},{2,50}... | collective-permute-start | bytes 1769480 | tf_op jit(solution)/shard_map/ppermute | solution.py:368
  134.5 14.6 %collective-permute-start.19 = (bf16[192,1536]{1,0:T(8,128)(2,1)}, bf16[192,1536]{1,0:T(8,128)(2,1)}, u32[]{:S(2)}, u32[]{:S(2)}) collective-permute-start(bf16[192,1536]{1,0:T(8,128)(2,1)} %get-tuple-element.95), channel_id=1, source_target_pairs={{0,16},{16,32},{32,48},{48,0},{1,17},{17,33},{33,49},{49,1},{2,18}... | collective-permute-start | bytes 1769480 | tf_op jit(solution)/shard_map/ppermute | solution.py:368
  142.7 20.1 %collective-permute-start.15 = (bf16[4,48,1152]{2,1,0:T(8,128)(2,1)}, bf16[4,48,1152]{2,1,0:T(8,128)(2,1)}, u32[]{:S(2)}, u32[]{:S(2)}) collective-permute-start(bf16[4,48,1152]{2,1,0:T(8,128)(2,1)} %get-tuple-element.100), channel_id=1, source_target_pairs={{0,2},{2,4},{4,6},{6,0},{1,3},{3,5},{5,7},{7,1},{8,10},{10,12},{12... | collective-permute-start | bytes 1327112 | tf_op jit(solution)/shard_map/ppermute | solution.py:368
  144.3 21.2 %collective-permute-start.16 = (bf16[4,48,1152]{2,1,0:T(8,128)(2,1)}, bf16[4,48,1152]{2,1,0:T(8,128)(2,1)}, u32[]{:S(2)}, u32[]{:S(2)}) collective-permute-start(bf16[4,48,1152]{2,1,0:T(8,128)(2,1)} %get-tuple-element.101), channel_id=1, source_target_pairs={{0,4},{2,6},{4,0},{6,2},{1,5},{3,7},{5,1},{7,3},{8,12},{10,14},{12... | collective-permute-start | bytes 1327112 | tf_op jit(solution)/shard_map/ppermute | solution.py:368
  147.6 18.9 %collective-permute-start.17 = (bf16[4,48,1152]{2,1,0:T(8,128)(2,1)}, bf16[4,48,1152]{2,1,0:T(8,128)(2,1)}, u32[]{:S(2)}, u32[]{:S(2)}) collective-permute-start(bf16[4,48,1152]{2,1,0:T(8,128)(2,1)} %get-tuple-element.102), channel_id=1, source_target_pairs={{0,6},{2,0},{4,2},{6,4},{1,7},{3,1},{5,3},{7,5},{8,14},{10,8},{12,... | collective-permute-start | bytes 1327112 | tf_op jit(solution)/shard_map/ppermute | solution.py:368
  160.1 26.9 %collective-permute-start.23 = (bf16[384,1536]{1,0:T(8,128)(2,1)}, bf16[384,1536]{1,0:T(8,128)(2,1)}, u32[]{:S(2)}, u32[]{:S(2)}) collective-permute-start(bf16[384,1536]{1,0:T(8,128)(2,1)} %get-tuple-element.111), channel_id=1, source_target_pairs={{0,16},{16,32},{32,48},{48,0},{1,17},{17,33},{33,49},{49,1},{2,18}... | collective-permute-start | bytes 3538952 | tf_op jit(solution)/shard_map/ppermute | solution.py:368
  160.3 26.7 %collective-permute-start.24 = (bf16[384,1536]{1,0:T(8,128)(2,1)}, bf16[384,1536]{1,0:T(8,128)(2,1)}, u32[]{:S(2)}, u32[]{:S(2)}) collective-permute-start(bf16[384,1536]{1,0:T(8,128)(2,1)} %get-tuple-element.112), channel_id=1, source_target_pairs={{0,48},{16,0},{32,16},{48,32},{1,49},{17,1},{33,17},{49,33},{2,50}... | collective-permute-start | bytes 3538952 | tf_op jit(solution)/shard_map/ppermute | solution.py:368
  168.9 12.9 %collective-permute-start.20 = (bf16[4,48,1152]{2,1,0:T(8,128)(2,1)}, bf16[4,48,1152]{2,1,0:T(8,128)(2,1)S(1)}, u32[]{:S(2)}, u32[]{:S(2)}) collective-permute-start(bf16[4,48,1152]{2,1,0:T(8,128)(2,1)} %shard_map.93), channel_id=1, source_target_pairs={{64,0},{72,8},{9,65},{1,73},{66,2},{74,10},{11,67},{3,75},{68,4},{... | collective-permute-start | bytes 1327112 | tf_op jit(solution)/shard_map/ppermute | solution.py:463
  173.3 8.5 %collective-permute-start.21 = (bf16[4,48,1152]{2,1,0:T(8,128)(2,1)}, bf16[4,48,1152]{2,1,0:T(8,128)(2,1)S(1)}, u32[]{:S(2)}, u32[]{:S(2)}) collective-permute-start(bf16[4,48,1152]{2,1,0:T(8,128)(2,1)} %shard_map.93), channel_id=1, source_target_pairs={{8,0},{0,8},{73,65},{65,73},{10,2},{2,10},{75,67},{67,75},{12,4},{... | collective-permute-start | bytes 1327112 | tf_op jit(solution)/shard_map/ppermute | solution.py:463
  174.0 13.1 %collective-permute-start.22 = (bf16[4,48,1152]{2,1,0:T(8,128)(2,1)}, bf16[4,48,1152]{2,1,0:T(8,128)(2,1)S(1)}, u32[]{:S(2)}, u32[]{:S(2)}) collective-permute-start(bf16[4,48,1152]{2,1,0:T(8,128)(2,1)} %shard_map.93), channel_id=1, source_target_pairs={{72,0},{64,8},{1,65},{9,73},{74,2},{66,10},{3,67},{11,75},{76,4},{... | collective-permute-start | bytes 1327112 | tf_op jit(solution)/shard_map/ppermute | solution.py:463
  177.1 13.3 %copy-start.2 = (bf16[384,1536]{1,0:T(8,128)(2,1)S(1)}, bf16[384,1536]{1,0:T(8,128)(2,1)}, u32[]{:S(2)}) copy-start(bf16[384,1536]{1,0:T(8,128)(2,1)} %get-tuple-element.106) | copy-start | bytes 3538948
  188.3 11.2 %collective-permute-start.27 = (bf16[48,1152]{1,0:T(8,128)(2,1)S(1)}, bf16[48,1152]{1,0:T(8,128)(2,1)S(1)}, u32[]{:S(2)}, u32[]{:S(2)}) collective-permute-start(bf16[48,1152]{1,0:T(8,128)(2,1)S(1)} %get-tuple-element.127), channel_id=1, source_target_pairs={{0,48},{16,0},{32,16},{48,32},{65,113},{81,65},{97,81},{113,97},{2... | collective-permute-start | bytes 331784 | tf_op jit(solution)/shard_map/ppermute | solution.py:377
  189.0 10.6 %collective-permute-start.26 = (bf16[48,1152]{1,0:T(8,128)(2,1)S(1)}, bf16[48,1152]{1,0:T(8,128)(2,1)S(1)}, u32[]{:S(2)}, u32[]{:S(2)}) collective-permute-start(bf16[48,1152]{1,0:T(8,128)(2,1)S(1)} %get-tuple-element.128), channel_id=1, source_target_pairs={{0,32},{16,48},{32,0},{48,16},{65,97},{81,113},{97,65},{113,81},{2... | collective-permute-start | bytes 331784 | tf_op jit(solution)/shard_map/ppermute | solution.py:377
  189.7 10.0 %collective-permute-start.25 = (bf16[48,1152]{1,0:T(8,128)(2,1)S(1)}, bf16[48,1152]{1,0:T(8,128)(2,1)S(1)}, u32[]{:S(2)}, u32[]{:S(2)}) collective-permute-start(bf16[48,1152]{1,0:T(8,128)(2,1)S(1)} %get-tuple-element.129), channel_id=1, source_target_pairs={{0,16},{16,32},{32,48},{48,0},{65,81},{81,97},{97,113},{113,65},{2... | collective-permute-start | bytes 331784 | tf_op jit(solution)/shard_map/ppermute | solution.py:377
  192.5 21.1 %collective-permute-start.31 = (bf16[384,1536]{1,0:T(8,128)(2,1)S(1)}, bf16[384,1536]{1,0:T(8,128)(2,1)S(1)}, u32[]{:S(2)}, u32[]{:S(2)}) collective-permute-start(bf16[384,1536]{1,0:T(8,128)(2,1)S(1)} %add_convert_fusion), channel_id=1, source_target_pairs={{1,64},{64,1},{3,66},{66,3},{5,68},{68,5},{7,70},{70,7},{9,72},{72... | collective-permute-start | bytes 3538952 | tf_op jit(solution)/shard_map/ppermute | solution.py:380
  199.9 2.3 %collective-permute-start.28 = (bf16[3,48,1536]{2,1,0:T(8,128)(2,1)S(1)}, bf16[3,48,1536]{2,1,0:T(8,128)(2,1)S(1)}, u32[]{:S(2)}, u32[]{:S(2)}) collective-permute-start(bf16[3,48,1536]{2,1,0:T(8,128)(2,1)S(1)} %maximum_dynamic-update-slice_fusion.3), channel_id=1, source_target_pairs={{0,2},{2,4},{4,6},{6,0},{65,67},{67,69},{69,71},{71,65},{8,10},{10... | collective-permute-start | bytes 1327112 | tf_op jit(solution)/shard_map/ppermute | solution.py:377
  200.7 1.6 collective-permute-start.29
  201.4 1.0 collective-permute-start.30
  213.6 16.9 %collective-permute-start.32 = (bf16[3,192,1536]{2,1,0:T(8,128)(2,1)S(1)}, bf16[3,192,1536]{2,1,0:T(8,128)(2,1)S(1)}, u32[]{:S(2)}, u32[]{:S(2)}) collective-permute-start(bf16[3,192,1536]{2,1,0:T(8,128)(2,1)S(1)} %constant_dynamic-update-slice_fusion), channel_id=1, source_target_pairs={{0,1},{65,64},{2,3},{67,66},{4,5},{69,68},{6,7},{71,70},{8,9},{73,... | collective-permute-start | bytes 5308424 | tf_op jit(solution)/shard_map/ppermute | solution.py:493
where the time goes:
time: 233 us; the launch traced here: 232 us
  Pallas kernels  91.1 us (39%)
  starting transfers between devices  60.8 us (26%)
  waiting for transfers between devices  57 us (24%)
  other arithmetic  15.1 us (6%)
  local copies, waits for them, and re-layouts  7.1 us (3%)
    pallas_call x1, Pallas kernels, attention(): pl.pallas_call(lambda *refs: attention_kernel(tok, nz, *refs), grid_spec=...  34.5 us
    pallas_call x4, Pallas kernels, place_block(): pl.pallas_call(lambda *refs: place_kernel(split, *refs), grid_spec=pltpu....  26.4 us
    pallas_call x2, Pallas kernels, input_grads(): pl.pallas_call(input_kernel, grid_spec=pltpu.PrefetchScalarGridSpec(num_s...  16.1 us
    ppermute x2, waiting for transfers between devices, swap_sides(): return lax.ppermute(value, ('xl', 'c'), [(1, 2), (2, 1)])  15.3 us
    ppermute x1, waiting for transfers between devices, on_device(): other = lax.ppermute(result, ('xl', 'c'), [(0, 1), (3, 2)])  14.4 us
    ppermute x10, starting transfers between devices, side_ring(): return lax.ppermute(value, ('xl', axis, 'c'), pairs)  14.1 us
    ppermute x9, starting transfers between devices, ring(): lax.ppermute(value, axis, [(i, (i + steps) % count) for i in range(count)])  12.9 us
    ppermute x2, starting transfers between devices, swap_sides(): return lax.ppermute(value, ('xl', 'c'), [(1, 2), (2, 1)])  11.5 us
  transfers between devices with their start and end apart: 33, of which 13 were waited for; matrix products, arithmetic and copies ran while one was open for 5% of the time, Pallas kernels for 22%

commit v1 on v0

--- a/solution.py
+++ b/solution.py
@@ -169,6 +169,37 @@
     )(index.reshape(1), w_query, w_key, w_value)
 
 
+def choose_kernel(place_ref, left_home, left_away, right_home, right_away, top_ref, low_ref):
+    @pl.when(place_ref[0] == 1)
+    def _():
+        top_ref[...] = left_home[...]
+        low_ref[...] = right_home[...]
+
+    @pl.when(place_ref[0] == 0)
+    def _():
+        top_ref[...] = left_away[...]
+        low_ref[...] = right_away[...]
+
+
+def choose(home, left_home, left_away, right_home, right_away):
+    half = left_home.shape[0] // 2
+    part = lambda side: pl.BlockSpec((half, D // 2), lambda n, place: (side, n))
+    return pl.pallas_call(
+        choose_kernel,
+        grid_spec=pltpu.PrefetchScalarGridSpec(
+            num_scalar_prefetch=1,
+            grid=(2,),
+            in_specs=[part(0), part(0), part(1), part(1)],
+            out_specs=[part(0), part(0)],
+        ),
+        out_shape=[jax.ShapeDtypeStruct((half, D), BF)] * 2,
+        compiler_params=pltpu.CompilerParams(vmem_limit_bytes=60 * 1024 * 1024),
+        cost_estimate=pl.CostEstimate(
+            flops=half * D, bytes_accessed=12 * half * D, transcendentals=0
+        ),
+    )(home.astype(jnp.int32).reshape(1), left_home, left_away, right_home, right_away)
+
+
 def place_kernel(split, place_ref, a_ref, b_ref, wkv_ref, wq_ref, *refs):
     t_ref, kv_ref, q_ref, block_ref = refs[-4:]
     step = pl.program_id(0)
@@ -280,11 +311,14 @@
     dkv = (dkv_ref[...].astype(F32) + extra).astype(BF)
     total = dot(dkv, wkv_ref[...], 1, 1) + dot(dq_ref[...], wq_ref[...], 1, 1)
     half = total.shape[0] // 2
+    if len(refs) == 1:
+        refs[0][...] = total.astype(BF)
+        return
     if len(refs) == 2:
         refs[0][...] = total[:half].astype(BF)
         refs[1][...] = total[half:].astype(BF)
         return
-    top_ref, low_ref, left_ref, right_ref, own_ref = refs
+    top_ref, low_ref, left_ref, right_ref = refs
 
     @pl.when(step == 0)
     def _():
@@ -296,17 +330,13 @@
         right_ref[:half, :] = total[:half].astype(BF)
         right_ref[half:, :] = (total[half:] + low_ref[...].astype(F32)).astype(BF)
 
-    @pl.when(step == 2)
-    def _():
-        own_ref[...] = total.astype(BF)
-
-
-def input_grads(blocks, dkv, extra, dq, weight_kv, weight_q, back=()):
+
+def input_grads(blocks, dkv, extra, dq, weight_kv, weight_q, heights, work, back=()):
     wide = dq.shape[1]
     tok = dq.shape[0] // 4
     rows = lambda cols: pl.BlockSpec((tok, cols), lambda n, place: (place[n], 0))
     whole = lambda rows, cols: pl.BlockSpec((rows, cols), lambda n, place: (0, 0))
-    made = [(tok, D)] * 3 if back else [(tok // 2, D)] * 2
+    made = [(height, D) for height in heights]
     return pl.pallas_call(
         input_kernel,
         grid_spec=pltpu.PrefetchScalarGridSpec(
@@ -323,27 +353,9 @@
         out_shape=[jax.ShapeDtypeStruct(shape, BF) for shape in made],
         compiler_params=pltpu.CompilerParams(vmem_limit_bytes=60 * 1024 * 1024),
         cost_estimate=pl.CostEstimate(
-            flops=FIRST, bytes_accessed=12 * 1024 * 1024, transcendentals=0
+            flops=work, bytes_accessed=12 * 1024 * 1024, transcendentals=0
         ),
     )(jnp.stack(blocks), dkv, extra, dq, weight_kv, weight_q, *back)
-
-
-def add_kernel(*refs):
-    total = refs[0][...].astype(F32)
-    for ref in refs[1:-1]:
-        total = total + ref[...].astype(F32)
-    refs[-1][...] = total.astype(BF)
-
-
-def add_up(parts, weight):
-    return pl.pallas_call(
-        add_kernel,
-        out_shape=jax.ShapeDtypeStruct(parts[0].shape, BF),
-        compiler_params=pltpu.CompilerParams(vmem_limit_bytes=60 * 1024 * 1024),
-        cost_estimate=pl.CostEstimate(
-            flops=512 * weight, bytes_accessed=weight, transcendentals=0
-        ),
-    )(*parts)
 
 
 def block_of(array, index, size):
@@ -410,14 +422,12 @@
     dout_far = crossed(cols(at(2)), 2)
     buffers = place_block((), own, moved, home, y, weight_kv, weight_q)
     dout_all = jnp.zeros((4 * tok, wide), BF)
-    for part, index in ((dout_own, y), (dout_left, at(-1)), (dout_right, at(1)), (dout_far, at(2))):
+    for part, index in ((dout_far, at(2)), (dout_left, at(-1)), (dout_right, at(1)), (dout_own, y)):
         dout_all = put(dout_all, part, index)
     buffers, dout_all, left_away, right_away = lax.optimization_barrier(
         (buffers, dout_all, left_away, right_away)
     )
-    far_top = jnp.where(home, left_home[:half], left_away[:half])
-    far_low = jnp.where(home, right_home[half:], right_away[half:])
-    far_top, far_low = lax.optimization_barrier((far_top, far_low))
+    far_top, far_low = choose(home, left_home, left_away, right_home, right_away)
     far_top = ring(far_top, "y", 1)
     far_low = ring(far_low, "y", -1)
     buffers = place_block(buffers, left_home, left_away, home, at(-1), weight_kv, weight_q)
@@ -435,21 +445,31 @@
     far_dhalo = lax.ppermute(dhalo, "c", [(1, 0)])
     got = lax.ppermute(give, "c", [(0, 1), (1, 0)])
     high = lax.ppermute(high, "c", [(0, 1)])
-    far_parts = input_grads([at(2)], dkv, far_dhalo, dq, weight_kv, weight_q)
+    far_parts = input_grads(
+        [at(2)], dkv, far_dhalo, dq, weight_kv, weight_q, (half, half), FIRST
+    )
     back_top = ring(far_parts[0], "y", -1)
     back_low = ring(far_parts[1], "y", 1)
     keep, far_parts = lax.optimization_barrier((keep, far_parts))
     slabs = list(finish(mine, nz, keep, got, low, high, dhalo, far_dhalo))
     sent = [ring(slabs[steps], "z", steps, nz) for steps in range(1, nz)]
     dkv, slabs[0] = lax.optimization_barrier((dkv, slabs[0]))
-    part_left, part_right, part_own = input_grads(
-        [at(-1), at(1), y], dkv, far_dhalo, dq, weight_kv, weight_q, (back_top, back_low)
+    part_left, part_right = input_grads(
+        [at(-1), at(1)], dkv, far_dhalo, dq, weight_kv, weight_q, (tok, tok), FIRST,
+        (back_top, back_low),
     )
     from_right = ring(part_left, "y", -1)
     from_left = ring(part_right, "y", 1)
-    *sent, part_own = lax.optimization_barrier((*sent, part_own))
-    share = add_up([slabs[0]] + sent, 4 * 1024 * 1024 * 1024)
-
+    *sent, part_left = lax.optimization_barrier((*sent, part_left))
+    share = slabs[0].astype(F32)
+    for part in sent:
+        share = share + part.astype(F32)
+    share = share.astype(BF)
+
+    dkv, share = lax.optimization_barrier((dkv, share))
+    (part_own,) = input_grads(
+        [y], dkv, far_dhalo, dq, weight_kv, weight_q, (tok,), 2 * tok * D * COLS
+    )
     around = 2 * nh
     arrived = []
     for steps in range(1, around):

time: 233 us -> 231 us (level)
  waiting for transfers between devices: 57 us -> 49.5 us
  local copies, waits for them, and re-layouts: 7.1 us -> 11.1 us
  other arithmetic: 15.1 us -> 11.4 us
  Pallas kernels: 91.1 us -> 94.1 us
    ppermute x3, waiting for transfers between devices: 9.88 us -> 2.9 us  [on_device(): arrived.append(lax.ppermute(share, ('xl', 'xh', 'c'), pairs))]
    ppermute x4, waiting for transfers between devices: 5.07 us -> 0.28 us  [crossed(): return lax.ppermute(value, ('xl', 'y', 'c'), pairs)]
    select_n x2 -> x0, other arithmetic: 4.26 us -> none  [the longest x1 2.14 us: on_device(): far_low = jnp.where(home, right_home[half:], right_away[half:])]
    dynamic_update_slice x3, local copies, waits for them, and re-layouts: 2.08 us -> 5.11 us  [put(): lax.dynamic_update_slice_in_dim(array, part, index * part.shape[0], 0)]
    pallas_call x2 -> x3, Pallas kernels: 16.1 us -> 19.1 us  [input_grads(): pl.pallas_call(input_kernel, grid_spec=pltpu.PrefetchScalarGridSpec(num_s...]
    ppermute x1, waiting for transfers between devices: 14.4 us -> 17.2 us  [on_device(): other = lax.ppermute(result, ('xl', 'c'), [(0, 1), (3, 2)])]
  transfers between devices with their start and end apart: 33 -> 33, of which waited for: 13 -> 11; matrix products, arithmetic and copies ran while one was open for 5% -> 7% of each run, Pallas kernels for 22% -> 22%
where the time goes in v1:
time: 231 us; the launch traced here: 230 us
  Pallas kernels  94.1 us (41%)
  starting transfers between devices  62.9 us (27%)
  waiting for transfers between devices  49.5 us (21%)
  other arithmetic  11.4 us (5%)
  local copies, waits for them, and re-layouts  11.1 us (5%)
    pallas_call x1, Pallas kernels, attention(): pl.pallas_call(lambda *refs: attention_kernel(tok, nz, *refs), grid_spec=...  34.5 us
    pallas_call x4, Pallas kernels, place_block(): pl.pallas_call(lambda *refs: place_kernel(split, *refs), grid_spec=pltpu....  26.5 us
    pallas_call x3, Pallas kernels, input_grads(): pl.pallas_call(input_kernel, grid_spec=pltpu.PrefetchScalarGridSpec(num_s...  19.1 us
    ppermute x1, waiting for transfers between devices, on_device(): other = lax.ppermute(result, ('xl', 'c'), [(0, 1), (3, 2)])  17.2 us
    ppermute x2, waiting for transfers between devices, swap_sides(): return lax.ppermute(value, ('xl', 'c'), [(1, 2), (2, 1)])  15.1 us
    ppermute x10, starting transfers between devices, side_ring(): return lax.ppermute(value, ('xl', axis, 'c'), pairs)  14.1 us
    ppermute x9, starting transfers between devices, ring(): lax.ppermute(value, axis, [(i, (i + steps) % count) for i in range(count)])  13 us
    ppermute x2, starting transfers between devices, swap_sides(): return lax.ppermute(value, ('xl', 'c'), [(1, 2), (2, 1)])  10.3 us
  transfers between devices with their start and end apart: 33, of which 11 were waited for; matrix products, arithmetic and copies ran while one was open for 7% of the time, Pallas kernels for 22%

profile of v1, /device:TPU:1, one launch (start us, length us, event | category | flops | bytes accessed | tf_op | source)
XLA Modules:
  0.0 230.1 jit_solution(18173374880869011732)
XLA Ops:
  0.6 4.5 %collective-permute-start = (bf16[384,1536]{1,0:T(8,128)(2,1)}, bf16[384,1536]{1,0:T(8,128)(2,1)}, u32[]{:S(2)}, u32[]{:S(2)}) collective-permute-start(bf16[384,1536]{1,0:T(8,128)(2,1)} %bitcast.68), channel_id=1, source_target_pairs={{1,64},{64,1},{3,66},{66,3},{5,68},{68,5},{7,70},{70,7},{9,72},{72... | collective-permute-start | bytes 3538952 | tf_op jit(solution)/shard_map/ppermute | solution.py:392
  5.2 1.7 collective-permute-start.1
  6.8 1.8 collective-permute-start.2
  8.6 4.9 %shard_map.84 = (bf16[1536,384]{1,0:T(8,128)(2,1)}, bf16[1536,768]{1,0:T(8,128)(2,1)}) custom-call(s32[1]{0:T(128)} %bitcast.place_ref, bf16[1536,1536]{1,0:T(8,128)(2,1)} %query_ref.1, bf16[1536,1536]{1,0:T(8,128)(2,1)} %key_ref.1, bf16[1536,1536]{1,0:T(8,128)(2,1)} %value_ref.1), custom_call_target="tpu_custom_call" | custom-call | flops 1099511627776 | bytes 7077888 | tf_op jit(solution)/shard_map/pallas_call | solution.py:150
  15.4 4.2 %collective-permute-done.refs_2_ = bf16[384,1536]{1,0:T(8,128)(2,1)} collective-permute-done((bf16[384,1536]{1,0:T(8,128)(2,1)}, bf16[384,1536]{1,0:T(8,128)(2,1)}, u32[]{:S(2)}, u32[]{:S(2)}) %collective-permute-start) | collective-permute-done | bytes 1179680 | tf_op jit(solution)/shard_map/ppermute | solution.py:392
  19.6 3.2 %collective-permute-start.7 = (bf16[384,1536]{1,0:T(8,128)(2,1)}, bf16[384,1536]{1,0:T(8,128)(2,1)}, u32[]{:S(2)}, u32[]{:S(2)}) collective-permute-start(bf16[384,1536]{1,0:T(8,128)(2,1)} %collective-permute-done.refs_2_), channel_id=1, source_target_pairs={{1,17},{17,33},{33,49},{49,1},{64,80},{80,96},{96,112},{112,64},{3... | collective-permute-start | bytes 3538952 | tf_op jit(solution)/shard_map/ppermute | solution.py:389
  22.8 3.4 %collective-permute-start.8 = (bf16[384,1536]{1,0:T(8,128)(2,1)}, bf16[384,1536]{1,0:T(8,128)(2,1)}, u32[]{:S(2)}, u32[]{:S(2)}) collective-permute-start(bf16[384,1536]{1,0:T(8,128)(2,1)} %collective-permute-done.refs_2_), channel_id=1, source_target_pairs={{1,49},{17,1},{33,17},{49,33},{64,112},{80,64},{96,80},{112,96},{3... | collective-permute-start | bytes 3538952 | tf_op jit(solution)/shard_map/ppermute | solution.py:389
  27.3 3.3 %collective-permute-start.3 = (bf16[384,384]{1,0:T(8,128)(2,1)}, bf16[384,384]{1,0:T(8,128)(2,1)}, u32[]{:S(2)}, u32[]{:S(2)}) collective-permute-start(bf16[384,384]{1,0:T(8,128)(2,1)} %get-tuple-element.126), channel_id=1, source_target_pairs={{0,32},{1,96},{16,48},{17,112},{32,0},{33,64},{48,16},{49,80},{64,... | collective-permute-start | bytes 884744 | tf_op jit(solution)/shard_map/ppermute | solution.py:405
  30.6 3.9 %collective-permute-start.5 = (bf16[384,384]{1,0:T(8,128)(2,1)}, bf16[384,384]{1,0:T(8,128)(2,1)}, u32[]{:S(2)}, u32[]{:S(2)}) collective-permute-start(bf16[384,384]{1,0:T(8,128)(2,1)} %get-tuple-element.124), channel_id=1, source_target_pairs={{0,48},{1,112},{16,0},{17,64},{32,16},{33,80},{48,32},{49,96},{64,... | collective-permute-start | bytes 884744 | tf_op jit(solution)/shard_map/ppermute | solution.py:405
  34.5 6.8 %shard_map.85 = (bf16[1536,1536]{1,0:T(8,128)(2,1)}, bf16[1536,768]{1,0:T(8,128)(2,1)}, bf16[1536,384]{1,0:T(8,128)(2,1)}) custom-call(s32[2]{0:T(128)} %pad_add_fusion.2.refs_0_, bf16[384,1536]{1,0:T(8,128)(2,1)} %bitcast.71, bf16[384,1536]{1,0:T(8,128)(2,1)} %collective-permute-done.refs_2_, bf16[1536,768]{1,0:T(8,128)(2,1)} %get-tuple-element.66.refs_3_.wkv_ref, ...), custom_call_target="tpu_custom_call" | custom-call | flops 1099511627776 | bytes 4718592 | tf_op jit(solution)/shard_map/pallas_call | solution.py:232
  41.3 1.9 collective-permute-start.6
  44.4 1.7 constant_dynamic-update-slice_fusion.6
  46.1 1.7 constant_dynamic-update-slice_fusion.5
  47.8 1.7 constant_dynamic-update-slice_fusion.4
  49.8 1.7 select_dynamic-update-slice_fusion.refs_5_
  51.5 1.2 collective-permute-done.8.right_away.refs_2_
  52.8 2.5 %shard_map.86 = (bf16[192,1536]{1,0:T(8,128)(2,1)}, bf16[192,1536]{1,0:T(8,128)(2,1)}) custom-call(s32[1]{0:T(128)} %bitcast.5.place_ref, bf16[384,1536]{1,0:T(8,128)(2,1)} %collective-permute-done.1.left_home.refs_1_, bf16[384,1536]{1,0:T(8,128)(2,1)} %collective-permute-done.7.left_away.refs_2_, ...), custom_call_target="tpu_custom_call" | custom-call | flops 294912 | bytes 3538944 | tf_op jit(solution)/shard_map/pallas_call | solution.py:187
  55.2 2.7 %collective-permute-start.10 = (bf16[192,1536]{1,0:T(8,128)(2,1)}, bf16[192,1536]{1,0:T(8,128)(2,1)}, u32[]{:S(2)}, u32[]{:S(2)}) collective-permute-start(bf16[192,1536]{1,0:T(8,128)(2,1)} %get-tuple-element.76), channel_id=1, source_target_pairs={{0,48},{16,0},{32,16},{48,32},{1,49},{17,1},{33,17},{49,33},{2,50}... | collective-permute-start | bytes 1769480 | tf_op jit(solution)/shard_map/ppermute | solution.py:380
  57.9 6.7 %shard_map.87 = (bf16[1536,1536]{1,0:T(8,128)(2,1)}, bf16[1536,768]{1,0:T(8,128)(2,1)}, bf16[1536,384]{1,0:T(8,128)(2,1)}) custom-call(s32[2]{0:T(128)} %pad_add_fusion.5.refs_0_, bf16[384,1536]{1,0:T(8,128)(2,1)} %collective-permute-done.1.left_home.refs_1_, ...), custom_call_target="tpu_custom_call", output_to_operand_aliasing={{0}: (5, {}), {1}: (6, {}), {2}: (7, {})} | custom-call | flops 1099511627776 | bytes 4718592 | tf_op jit(solution)/shard_map/pallas_call | solution.py:232
  64.6 6.7 %shard_map.88 = (bf16[1536,1536]{1,0:T(8,128)(2,1)}, bf16[1536,768]{1,0:T(8,128)(2,1)}, bf16[1536,384]{1,0:T(8,128)(2,1)}) custom-call(s32[2]{0:T(128)} %get-tuple-element.168.refs_0_, bf16[384,1536]{1,0:T(8,128)(2,1)} %collective-permute-done.2.right_home.refs_1_, ...), custom_call_target="tpu_custom_call", output_to_operand_aliasing={{0}: (5, {}), {1}: (6, {}), {2}: (7, {})} | custom-call | flops 1099511627776 | bytes 4718592 | tf_op jit(solution)/shard_map/pallas_call | solution.py:232
  71.3 6.2 %shard_map.89 = (bf16[1536,1536]{1,0:T(8,128)(2,1)}, bf16[1536,768]{1,0:T(8,128)(2,1)}, bf16[1536,384]{1,0:T(8,128)(2,1)}) custom-call(s32[2]{0:T(128)} %get-tuple-element.167.refs_0_, bf16[192,1536]{1,0:T(8,128)(2,1)} %collective-permute-done.9.refs_1_, ...), custom_call_target="tpu_custom_call", output_to_operand_aliasing={{0}: (5, {}), {1}: (6, {}), {2}: (7, {})} | custom-call | flops 1099511627776 | bytes 4718592 | tf_op jit(solution)/shard_map/pallas_call | solution.py:232
  77.5 1.3 slice.129
  78.9 1.5 collective-permute-start.11
  81.0 5.4 %collective-permute-done.11.refs_4_ = bf16[768,768]{1,0:T(8,128)(2,1)S(1)} collective-permute-done((bf16[768,768]{1,0:T(8,128)(2,1)S(1)}, bf16[768,768]{1,0:T(8,128)(2,1)S(1)}, u32[]{:S(2)}, u32[]{:S(2)}) %collective-permute-start.11) | collective-permute-done | bytes 1179680 | tf_op jit(solution)/shard_map/ppermute | solution.py:439
  87.4 34.5 %shard_map.90 = (bf16[1536,384]{1,0:T(8,128)(2,1)}, bf16[1536,768]{1,0:T(8,128)(2,1)}, bf16[768,768]{1,0:T(8,128)(2,1)}, bf16[4,4,48,1152]{3,2,1,0:T(8,128)(2,1)...) custom-call(s32[2]{0:T(128)} %pad_add_fusion.refs_0_, ...), custom_call_target="tpu_custom_call" | custom-call | flops 19025362944 | bytes 28311552 | tf_op jit(solution)/shard_map/pallas_call | solution.py:112
  121.8 2.1 collective-permute-start.12
  124.6 1.3 collective-permute-start.14
  127.6 5.1 %shard_map.91 = (bf16[192,1536]{1,0:T(8,128)(2,1)}, bf16[192,1536]{1,0:T(8,128)(2,1)}) custom-call(s32[1]{0:T(128)} %bitcast.4.place_ref, bf16[1536,768]{1,0:T(8,128)(2,1)} %get-tuple-element.110.dkv_ref, bf16[768,768]{1,0:T(8,128)(2,1)} %copy-done.2, bf16[1536,384]{1,0:T(8,128)(2,1)} %get-tuple-element.93.dq_ref, ...), custom_call_target="tpu_custom_call" | custom-call | flops 1099511627776 | bytes 12582912 | tf_op jit(solution)/shard_map/pallas_call | solution.py:340
  132.7 2.0 collective-permute-start.18
  134.6 6.7 %shard_map.92 = (bf16[4,48,1152]{2,1,0:T(8,128)(2,1)}, bf16[4,48,1152]{2,1,0:T(8,128)(2,1)}, bf16[4,48,1152]{2,1,0:T(8,128)(2,1)}, bf16[4,48,1152]{2,1,0:T(8,128)(2,1)}) custom-call(s32[2]{0:T(128)} %pad_add_fusion.refs_0_, bf16[4,4,48,1152]{3,2,1,0:T(8,128)(2,1)} %get-tuple-element.96.refs_1_, bf16[4,4,48,1152]{3,2,1,0:T(8,128)(2,1)} %collective-permute-done.13.refs_2_, ...), custom_call_target="tpu_custom_call" | custom-call | flops 1099511627776 | bytes 12582912 | tf_op jit(solution)/shard_map/pallas_call | solution.py:290
  141.3 1.7 collective-permute-start.15
  143.0 3.3 %collective-permute-start.16 = (bf16[4,48,1152]{2,1,0:T(8,128)(2,1)}, bf16[4,48,1152]{2,1,0:T(8,128)(2,1)}, u32[]{:S(2)}, u32[]{:S(2)}) collective-permute-start(bf16[4,48,1152]{2,1,0:T(8,128)(2,1)} %get-tuple-element.104), channel_id=1, source_target_pairs={{0,4},{2,6},{4,0},{6,2},{1,5},{3,7},{5,1},{7,3},{8,12},{10,14},{12... | collective-permute-start | bytes 1327112 | tf_op jit(solution)/shard_map/ppermute | solution.py:380
  147.0 2.1 collective-permute-done.19.refs_1_
  149.1 8.8 %shard_map.93 = (bf16[384,1536]{1,0:T(8,128)(2,1)}, bf16[384,1536]{1,0:T(8,128)(2,1)}) custom-call(s32[2]{0:T(128)} %pad_add_fusion.4.place_ref, bf16[1536,768]{1,0:T(8,128)(2,1)} %get-tuple-element.110.dkv_ref, bf16[768,768]{1,0:T(8,128)(2,1)} %copy-done.2, bf16[1536,384]{1,0:T(8,128)(2,1)} %get-tuple-element.93.dq_ref, ...), custom_call_target="tpu_custom_call" | custom-call | flops 1099511627776 | bytes 12582912 | tf_op jit(solution)/shard_map/pallas_call | solution.py:340
  157.9 2.7 %collective-permute-start.24 = (bf16[384,1536]{1,0:T(8,128)(2,1)}, bf16[384,1536]{1,0:T(8,128)(2,1)S(1)}, u32[]{:S(2)}, u32[]{:S(2)}) collective-permute-start(bf16[384,1536]{1,0:T(8,128)(2,1)} %get-tuple-element.106), channel_id=1, source_target_pairs={{0,48},{16,0},{32,16},{48,32},{1,49},{17,1},{33,17},{49,33},{2,50}... | collective-permute-start | bytes 3538952 | tf_op jit(solution)/shard_map/ppermute | solution.py:380
  160.6 3.9 %collective-permute-done.16 = bf16[4,48,1152]{2,1,0:T(8,128)(2,1)} collective-permute-done((bf16[4,48,1152]{2,1,0:T(8,128)(2,1)}, bf16[4,48,1152]{2,1,0:T(8,128)(2,1)}, u32[]{:S(2)}, u32[]{:S(2)}) %collective-permute-start.16) | collective-permute-done | bytes 442400 | tf_op jit(solution)/shard_map/ppermute | solution.py:380
  165.2 1.5 add_convert_fusion.2
  166.7 5.7 %collective-permute-start.20 = (bf16[4,48,1152]{2,1,0:T(8,128)(2,1)S(1)}, bf16[4,48,1152]{2,1,0:T(8,128)(2,1)S(1)}, u32[]{:S(2)}, u32[]{:S(2)}) collective-permute-start(bf16[4,48,1152]{2,1,0:T(8,128)(2,1)S(1)} %add_convert_fusion.2), channel_id=1, source_target_pairs={{64,0},{72,8},{9,65},{1,73},{66,2},{74,10},{11,67},{3,75},{68,4},{... | collective-permute-start | bytes 1327112 | tf_op jit(solution)/shard_map/ppermute | solution.py:483
  172.4 1.4 collective-permute-start.21
  173.9 3.1 %collective-permute-start.22 = (bf16[4,48,1152]{2,1,0:T(8,128)(2,1)S(1)}, bf16[4,48,1152]{2,1,0:T(8,128)(2,1)}, u32[]{:S(2)}, u32[]{:S(2)}) collective-permute-start(bf16[4,48,1152]{2,1,0:T(8,128)(2,1)S(1)} %add_convert_fusion.2), channel_id=1, source_target_pairs={{72,0},{64,8},{1,65},{9,73},{74,2},{66,10},{3,67},{11,75},{76,4},{... | collective-permute-start | bytes 1327112 | tf_op jit(solution)/shard_map/ppermute | solution.py:483
  177.0 5.2 %shard_map.94 = bf16[384,1536]{1,0:T(8,128)(2,1)} custom-call(s32[1]{0:T(128)} %bitcast.place_ref, bf16[1536,768]{1,0:T(8,128)(2,1)} %get-tuple-element.110.dkv_ref, bf16[768,768]{1,0:T(8,128)(2,1)} %copy-done.2, bf16[1536,384]{1,0:T(8,128)(2,1)} %get-tuple-element.93.dq_ref, bf16[1536,768]{1,0:T(8,128)(2,1)} %get-tuple-element.66.refs_3_.wkv_ref, ...), custom_call_target="tpu_custom_call" | custom-call | flops 1358954496 | bytes 12582912 | tf_op jit(solution)/shard_map/pallas_call | solution.py:340
  182.2 2.9 %collective-permute-done.22 = bf16[4,48,1152]{2,1,0:T(8,128)(2,1)} collective-permute-done((bf16[4,48,1152]{2,1,0:T(8,128)(2,1)S(1)}, bf16[4,48,1152]{2,1,0:T(8,128)(2,1)}, u32[]{:S(2)}, u32[]{:S(2)}) %collective-permute-start.22) | collective-permute-done | bytes 442400 | tf_op jit(solution)/shard_map/ppermute | solution.py:483
  185.1 1.4 add_convert_fusion.1
  189.0 5.8 %collective-permute-start.31 = (bf16[384,1536]{1,0:T(8,128)(2,1)S(1)}, bf16[384,1536]{1,0:T(8,128)(2,1)S(1)}, u32[]{:S(2)}, u32[]{:S(2)}) collective-permute-start(bf16[384,1536]{1,0:T(8,128)(2,1)S(1)} %add_convert_fusion), channel_id=1, source_target_pairs={{1,64},{64,1},{3,66},{66,3},{5,68},{68,5},{7,70},{70,7},{9,72},{72... | collective-permute-start | bytes 3538952 | tf_op jit(solution)/shard_map/ppermute | solution.py:392
  197.8 10.9 %collective-permute-done.31 = bf16[384,1536]{1,0:T(8,128)(2,1)S(1)} collective-permute-done((bf16[384,1536]{1,0:T(8,128)(2,1)S(1)}, bf16[384,1536]{1,0:T(8,128)(2,1)S(1)}, u32[]{:S(2)}, u32[]{:S(2)}) %collective-permute-start.31) | collective-permute-done | bytes 1179680 | tf_op jit(solution)/shard_map/ppermute | solution.py:392
  208.7 1.3 collective-permute-start.32
  211.1 17.2 %collective-permute-done.32 = bf16[3,192,1536]{2,1,0:T(8,128)(2,1)S(1)} collective-permute-done((bf16[3,192,1536]{2,1,0:T(8,128)(2,1)S(1)}, bf16[3,192,1536]{2,1,0:T(8,128)(2,1)S(1)}, u32[]{:S(2)}, u32[]{:S(2)}) %collective-permute-start.32) | collective-permute-done | bytes 1769504 | tf_op jit(solution)/shard_map/ppermute | solution.py:513
  228.3 1.9 fusion.1
  (85 shorter events, 16.2 us)
Async XLA Ops:
  0.6 19.0 %collective-permute-start = (bf16[384,1536]{1,0:T(8,128)(2,1)}, bf16[384,1536]{1,0:T(8,128)(2,1)}, u32[]{:S(2)}, u32[]{:S(2)}) collective-permute-start(bf16[384,1536]{1,0:T(8,128)(2,1)} %bitcast.68), channel_id=1, source_target_pairs={{1,64},{64,1},{3,66},{66,3},{5,68},{68,5},{7,70},{70,7},{9,72},{72... | collective-permute-start | bytes 3538952 | tf_op jit(solution)/shard_map/ppermute | solution.py:392
  5.2 14.5 %collective-permute-start.1 = (bf16[384,1536]{1,0:T(8,128)(2,1)}, bf16[384,1536]{1,0:T(8,128)(2,1)}, u32[]{:S(2)}, u32[]{:S(2)}) collective-permute-start(bf16[384,1536]{1,0:T(8,128)(2,1)} %bitcast.69), channel_id=1, source_target_pairs={{0,16},{16,32},{32,48},{48,0},{65,81},{81,97},{97,113},{113,65},{2... | collective-permute-start | bytes 3538952 | tf_op jit(solution)/shard_map/ppermute | solution.py:389
  6.8 12.8 %collective-permute-start.2 = (bf16[384,1536]{1,0:T(8,128)(2,1)}, bf16[384,1536]{1,0:T(8,128)(2,1)}, u32[]{:S(2)}, u32[]{:S(2)}) collective-permute-start(bf16[384,1536]{1,0:T(8,128)(2,1)} %bitcast.70), channel_id=1, source_target_pairs={{0,48},{16,0},{32,16},{48,32},{65,113},{81,65},{97,81},{113,97},{2... | collective-permute-start | bytes 3538952 | tf_op jit(solution)/shard_map/ppermute | solution.py:389
  8.6 17.6 %copy-start.1 = (bf16[1,384,1536]{2,1,0:T(8,128)(2,1)S(1)}, bf16[1,384,1536]{2,1,0:T(8,128)(2,1)}, u32[]{:S(2)}) copy-start(bf16[1,384,1536]{2,1,0:T(8,128)(2,1)} %param.9) | copy-start | bytes 3538948
  19.6 31.9 %collective-permute-start.7 = (bf16[384,1536]{1,0:T(8,128)(2,1)}, bf16[384,1536]{1,0:T(8,128)(2,1)}, u32[]{:S(2)}, u32[]{:S(2)}) collective-permute-start(bf16[384,1536]{1,0:T(8,128)(2,1)} %collective-permute-done.refs_2_), channel_id=1, source_target_pairs={{1,17},{17,33},{33,49},{49,1},{64,80},{80,96},{96,112},{112,64},{3... | collective-permute-start | bytes 3538952 | tf_op jit(solution)/shard_map/ppermute | solution.py:389
  22.8 29.9 %collective-permute-start.8 = (bf16[384,1536]{1,0:T(8,128)(2,1)}, bf16[384,1536]{1,0:T(8,128)(2,1)}, u32[]{:S(2)}, u32[]{:S(2)}) collective-permute-start(bf16[384,1536]{1,0:T(8,128)(2,1)} %collective-permute-done.refs_2_), channel_id=1, source_target_pairs={{1,49},{17,1},{33,17},{49,33},{64,112},{80,64},{96,80},{112,96},{3... | collective-permute-start | bytes 3538952 | tf_op jit(solution)/shard_map/ppermute | solution.py:389
  27.3 14.0 %collective-permute-start.3 = (bf16[384,384]{1,0:T(8,128)(2,1)}, bf16[384,384]{1,0:T(8,128)(2,1)}, u32[]{:S(2)}, u32[]{:S(2)}) collective-permute-start(bf16[384,384]{1,0:T(8,128)(2,1)} %get-tuple-element.126), channel_id=1, source_target_pairs={{0,32},{1,96},{16,48},{17,112},{32,0},{33,64},{48,16},{49,80},{64,... | collective-permute-start | bytes 884744 | tf_op jit(solution)/shard_map/ppermute | solution.py:405
  30.6 15.5 %collective-permute-start.4 = (bf16[384,384]{1,0:T(8,128)(2,1)}, bf16[384,384]{1,0:T(8,128)(2,1)}, u32[]{:S(2)}, u32[]{:S(2)}) collective-permute-start(bf16[384,384]{1,0:T(8,128)(2,1)} %get-tuple-element.125), channel_id=1, source_target_pairs={{0,16},{1,80},{16,32},{17,96},{32,48},{33,112},{48,0},{49,64},{64,... | collective-permute-start | bytes 884744 | tf_op jit(solution)/shard_map/ppermute | solution.py:405
  30.6 17.2 %collective-permute-start.5 = (bf16[384,384]{1,0:T(8,128)(2,1)}, bf16[384,384]{1,0:T(8,128)(2,1)}, u32[]{:S(2)}, u32[]{:S(2)}) collective-permute-start(bf16[384,384]{1,0:T(8,128)(2,1)} %get-tuple-element.124), channel_id=1, source_target_pairs={{0,48},{1,112},{16,0},{17,64},{32,16},{33,80},{48,32},{49,96},{64,... | collective-permute-start | bytes 884744 | tf_op jit(solution)/shard_map/ppermute | solution.py:405
  34.5 6.8 %copy-start.4 = (bf16[384,384]{1,0:T(8,128)(2,1)S(1)}, bf16[384,384]{1,0:T(8,128)(2,1)}, u32[]{:S(2)}) copy-start(bf16[384,384]{1,0:T(8,128)(2,1)} %get-tuple-element.123) | copy-start | bytes 884740
  41.3 8.4 %collective-permute-start.6 = (bf16[384,384]{1,0:T(8,128)(2,1)S(1)}, bf16[384,384]{1,0:T(8,128)(2,1)S(1)}, u32[]{:S(2)}, u32[]{:S(2)}) collective-permute-start(bf16[384,384]{1,0:T(8,128)(2,1)S(1)} %copy-done.4), channel_id=1, source_target_pairs={{1,64},{17,80},{33,96},{49,112},{64,1},{80,17},{96,33},{112,49},{3... | collective-permute-start | bytes 884744 | tf_op jit(solution)/shard_map/ppermute | solution.py:405
  55.2 16.1 %collective-permute-start.10 = (bf16[192,1536]{1,0:T(8,128)(2,1)}, bf16[192,1536]{1,0:T(8,128)(2,1)}, u32[]{:S(2)}, u32[]{:S(2)}) collective-permute-start(bf16[192,1536]{1,0:T(8,128)(2,1)} %get-tuple-element.76), channel_id=1, source_target_pairs={{0,48},{16,0},{32,16},{48,32},{1,49},{17,1},{33,17},{49,33},{2,50}... | collective-permute-start | bytes 1769480 | tf_op jit(solution)/shard_map/ppermute | solution.py:380
  57.9 13.4 %collective-permute-start.9 = (bf16[192,1536]{1,0:T(8,128)(2,1)}, bf16[192,1536]{1,0:T(8,128)(2,1)}, u32[]{:S(2)}, u32[]{:S(2)}) collective-permute-start(bf16[192,1536]{1,0:T(8,128)(2,1)} %get-tuple-element.75), channel_id=1, source_target_pairs={{0,16},{16,32},{32,48},{48,0},{1,17},{17,33},{33,49},{49,1},{2,18}... | collective-permute-start | bytes 1769480 | tf_op jit(solution)/shard_map/ppermute | solution.py:380
  78.9 7.5 %collective-permute-start.11 = (bf16[768,768]{1,0:T(8,128)(2,1)S(1)}, bf16[768,768]{1,0:T(8,128)(2,1)S(1)}, u32[]{:S(2)}, u32[]{:S(2)}) collective-permute-start(bf16[768,768]{1,0:T(8,128)(2,1)S(1)} %slice.129), channel_id=1, source_target_pairs={{0,1},{2,3},{4,5},{6,7},{8,9},{10,11},{12,13},{14,15},{16,17},{18,... | collective-permute-start | bytes 3538952 | tf_op jit(solution)/shard_map/ppermute | solution.py:439
  86.4 1.0 copy-start.5
  121.8 4.7 %collective-permute-start.12 = (bf16[768,768]{1,0:T(8,128)(2,1)}, bf16[768,768]{1,0:T(8,128)(2,1)S(1)}, u32[]{:S(2)}, u32[]{:S(2)}) collective-permute-start(bf16[768,768]{1,0:T(8,128)(2,1)} %get-tuple-element.92.refs_5_), channel_id=1, source_target_pairs={{1,0},{3,2},{5,4},{7,6},{9,8},{11,10},{13,12},{15,14},{17,16},{19,... | collective-permute-start | bytes 3538952 | tf_op jit(solution)/shard_map/ppermute | solution.py:445
  124.6 10.0 %collective-permute-start.13 = (bf16[4,4,48,1152]{3,2,1,0:T(8,128)(2,1)}, bf16[4,4,48,1152]{3,2,1,0:T(8,128)(2,1)}, u32[]{:S(2)}, u32[]{:S(2)}) collective-permute-start(bf16[4,4,48,1152]{3,2,1,0:T(8,128)(2,1)} %get-tuple-element.97), channel_id=1, source_target_pairs={{0,1},{1,0},{2,3},{3,2},{4,5},{5,4},{6,7},{7,6},{8,9},{9,8},{10,11... | collective-permute-start | bytes 5308424 | tf_op jit(solution)/shard_map/ppermute | solution.py:446
  124.6 10.0 %collective-permute-start.14 = (bf16[768,768]{1,0:T(8,128)(2,1)}, bf16[768,768]{1,0:T(8,128)(2,1)}, u32[]{:S(2)}, u32[]{:S(2)}) collective-permute-start(bf16[768,768]{1,0:T(8,128)(2,1)} %get-tuple-element.99), channel_id=1, source_target_pairs={{0,1},{2,3},{4,5},{6,7},{8,9},{10,11},{12,13},{14,15},{16,17},{18,... | collective-permute-start | bytes 3538952 | tf_op jit(solution)/shard_map/ppermute | solution.py:447
  126.6 1.0 copy-start.2
  132.7 14.4 %collective-permute-start.18 = (bf16[192,1536]{1,0:T(8,128)(2,1)}, bf16[192,1536]{1,0:T(8,128)(2,1)}, u32[]{:S(2)}, u32[]{:S(2)}) collective-permute-start(bf16[192,1536]{1,0:T(8,128)(2,1)} %get-tuple-element.94), channel_id=1, source_target_pairs={{0,48},{16,0},{32,16},{48,32},{1,49},{17,1},{33,17},{49,33},{2,50}... | collective-permute-start | bytes 1769480 | tf_op jit(solution)/shard_map/ppermute | solution.py:380
  134.6 14.5 %collective-permute-start.19 = (bf16[192,1536]{1,0:T(8,128)(2,1)}, bf16[192,1536]{1,0:T(8,128)(2,1)}, u32[]{:S(2)}, u32[]{:S(2)}) collective-permute-start(bf16[192,1536]{1,0:T(8,128)(2,1)} %get-tuple-element.95), channel_id=1, source_target_pairs={{0,16},{16,32},{32,48},{48,0},{1,17},{17,33},{33,49},{49,1},{2,18}... | collective-permute-start | bytes 1769480 | tf_op jit(solution)/shard_map/ppermute | solution.py:380
  141.3 19.3 %collective-permute-start.15 = (bf16[4,48,1152]{2,1,0:T(8,128)(2,1)}, bf16[4,48,1152]{2,1,0:T(8,128)(2,1)}, u32[]{:S(2)}, u32[]{:S(2)}) collective-permute-start(bf16[4,48,1152]{2,1,0:T(8,128)(2,1)} %get-tuple-element.103), channel_id=1, source_target_pairs={{0,2},{2,4},{4,6},{6,0},{1,3},{3,5},{5,7},{7,1},{8,10},{10,12},{12... | collective-permute-start | bytes 1327112 | tf_op jit(solution)/shard_map/ppermute | solution.py:380
  143.0 21.4 %collective-permute-start.16 = (bf16[4,48,1152]{2,1,0:T(8,128)(2,1)}, bf16[4,48,1152]{2,1,0:T(8,128)(2,1)}, u32[]{:S(2)}, u32[]{:S(2)}) collective-permute-start(bf16[4,48,1152]{2,1,0:T(8,128)(2,1)} %get-tuple-element.104), channel_id=1, source_target_pairs={{0,4},{2,6},{4,0},{6,2},{1,5},{3,7},{5,1},{7,3},{8,12},{10,14},{12... | collective-permute-start | bytes 1327112 | tf_op jit(solution)/shard_map/ppermute | solution.py:380
  146.3 18.9 %collective-permute-start.17 = (bf16[4,48,1152]{2,1,0:T(8,128)(2,1)}, bf16[4,48,1152]{2,1,0:T(8,128)(2,1)}, u32[]{:S(2)}, u32[]{:S(2)}) collective-permute-start(bf16[4,48,1152]{2,1,0:T(8,128)(2,1)} %get-tuple-element.105), channel_id=1, source_target_pairs={{0,6},{2,0},{4,2},{6,4},{1,7},{3,1},{5,3},{7,5},{8,14},{10,8},{12,... | collective-permute-start | bytes 1327112 | tf_op jit(solution)/shard_map/ppermute | solution.py:380
  149.1 16.1 %copy-start.3 = (bf16[4,48,1152]{2,1,0:T(8,128)(2,1)S(1)}, bf16[4,48,1152]{2,1,0:T(8,128)(2,1)}, u32[]{:S(2)}) copy-start(bf16[4,48,1152]{2,1,0:T(8,128)(2,1)} %get-tuple-element.102) | copy-start | bytes 1327108
  157.9 27.2 %collective-permute-start.23 = (bf16[384,1536]{1,0:T(8,128)(2,1)}, bf16[384,1536]{1,0:T(8,128)(2,1)S(1)}, u32[]{:S(2)}, u32[]{:S(2)}) collective-permute-start(bf16[384,1536]{1,0:T(8,128)(2,1)} %get-tuple-element.112), channel_id=1, source_target_pairs={{0,16},{16,32},{32,48},{48,0},{1,17},{17,33},{33,49},{49,1},{2,18}... | collective-permute-start | bytes 3538952 | tf_op jit(solution)/shard_map/ppermute | solution.py:380
  157.9 27.2 %collective-permute-start.24 = (bf16[384,1536]{1,0:T(8,128)(2,1)}, bf16[384,1536]{1,0:T(8,128)(2,1)S(1)}, u32[]{:S(2)}, u32[]{:S(2)}) collective-permute-start(bf16[384,1536]{1,0:T(8,128)(2,1)} %get-tuple-element.106), channel_id=1, source_target_pairs={{0,48},{16,0},{32,16},{48,32},{1,49},{17,1},{33,17},{49,33},{2,50}... | collective-permute-start | bytes 3538952 | tf_op jit(solution)/shard_map/ppermute | solution.py:380
  166.7 15.5 %collective-permute-start.20 = (bf16[4,48,1152]{2,1,0:T(8,128)(2,1)S(1)}, bf16[4,48,1152]{2,1,0:T(8,128)(2,1)S(1)}, u32[]{:S(2)}, u32[]{:S(2)}) collective-permute-start(bf16[4,48,1152]{2,1,0:T(8,128)(2,1)S(1)} %add_convert_fusion.2), channel_id=1, source_target_pairs={{64,0},{72,8},{9,65},{1,73},{66,2},{74,10},{11,67},{3,75},{68,4},{... | collective-permute-start | bytes 1327112 | tf_op jit(solution)/shard_map/ppermute | solution.py:483
  172.4 9.8 %collective-permute-start.21 = (bf16[4,48,1152]{2,1,0:T(8,128)(2,1)S(1)}, bf16[4,48,1152]{2,1,0:T(8,128)(2,1)}, u32[]{:S(2)}, u32[]{:S(2)}) collective-permute-start(bf16[4,48,1152]{2,1,0:T(8,128)(2,1)S(1)} %add_convert_fusion.2), channel_id=1, source_target_pairs={{8,0},{0,8},{73,65},{65,73},{10,2},{2,10},{75,67},{67,75},{12,4},{... | collective-permute-start | bytes 1327112 | tf_op jit(solution)/shard_map/ppermute | solution.py:483
  173.9 11.2 %collective-permute-start.22 = (bf16[4,48,1152]{2,1,0:T(8,128)(2,1)S(1)}, bf16[4,48,1152]{2,1,0:T(8,128)(2,1)}, u32[]{:S(2)}, u32[]{:S(2)}) collective-permute-start(bf16[4,48,1152]{2,1,0:T(8,128)(2,1)S(1)} %add_convert_fusion.2), channel_id=1, source_target_pairs={{72,0},{64,8},{1,65},{9,73},{74,2},{66,10},{3,67},{11,75},{76,4},{... | collective-permute-start | bytes 1327112 | tf_op jit(solution)/shard_map/ppermute | solution.py:483
  182.2 6.4 %copy-start = (bf16[384,1536]{1,0:T(8,128)(2,1)S(1)}, bf16[384,1536]{1,0:T(8,128)(2,1)}, u32[]{:S(2)}) copy-start(bf16[384,1536]{1,0:T(8,128)(2,1)} %shard_map.94) | copy-start | bytes 3538948
  186.5 8.4 %collective-permute-start.27 = (bf16[48,1152]{1,0:T(8,128)(2,1)S(1)}, bf16[48,1152]{1,0:T(8,128)(2,1)S(1)}, u32[]{:S(2)}, u32[]{:S(2)}) collective-permute-start(bf16[48,1152]{1,0:T(8,128)(2,1)S(1)} %get-tuple-element.127), channel_id=1, source_target_pairs={{0,48},{16,0},{32,16},{48,32},{65,113},{81,65},{97,81},{113,97},{2... | collective-permute-start | bytes 331784 | tf_op jit(solution)/shard_map/ppermute | solution.py:389
  187.2 7.8 %collective-permute-start.26 = (bf16[48,1152]{1,0:T(8,128)(2,1)S(1)}, bf16[48,1152]{1,0:T(8,128)(2,1)S(1)}, u32[]{:S(2)}, u32[]{:S(2)}) collective-permute-start(bf16[48,1152]{1,0:T(8,128)(2,1)S(1)} %get-tuple-element.128), channel_id=1, source_target_pairs={{0,32},{16,48},{32,0},{48,16},{65,97},{81,113},{97,65},{113,81},{2... | collective-permute-start | bytes 331784 | tf_op jit(solution)/shard_map/ppermute | solution.py:389
  187.9 7.2 %collective-permute-start.25 = (bf16[48,1152]{1,0:T(8,128)(2,1)S(1)}, bf16[48,1152]{1,0:T(8,128)(2,1)S(1)}, u32[]{:S(2)}, u32[]{:S(2)}) collective-permute-start(bf16[48,1152]{1,0:T(8,128)(2,1)S(1)} %get-tuple-element.129), channel_id=1, source_target_pairs={{0,16},{16,32},{32,48},{48,0},{65,81},{81,97},{97,113},{113,65},{2... | collective-permute-start | bytes 331784 | tf_op jit(solution)/shard_map/ppermute | solution.py:389
  189.0 19.6 %collective-permute-start.31 = (bf16[384,1536]{1,0:T(8,128)(2,1)S(1)}, bf16[384,1536]{1,0:T(8,128)(2,1)S(1)}, u32[]{:S(2)}, u32[]{:S(2)}) collective-permute-start(bf16[384,1536]{1,0:T(8,128)(2,1)S(1)} %add_convert_fusion), channel_id=1, source_target_pairs={{1,64},{64,1},{3,66},{66,3},{5,68},{68,5},{7,70},{70,7},{9,72},{72... | collective-permute-start | bytes 3538952 | tf_op jit(solution)/shard_map/ppermute | solution.py:392
  195.3 2.3 %collective-permute-start.28 = (bf16[3,48,1536]{2,1,0:T(8,128)(2,1)S(1)}, bf16[3,48,1536]{2,1,0:T(8,128)(2,1)S(1)}, u32[]{:S(2)}, u32[]{:S(2)}) collective-permute-start(bf16[3,48,1536]{2,1,0:T(8,128)(2,1)S(1)} %maximum_dynamic-update-slice_fusion.3), channel_id=1, source_target_pairs={{0,2},{2,4},{4,6},{6,0},{65,67},{67,69},{69,71},{71,65},{8,10},{10... | collective-permute-start | bytes 1327112 | tf_op jit(solution)/shard_map/ppermute | solution.py:389
  196.0 1.6 collective-permute-start.29
  196.7 1.0 collective-permute-start.30
  208.7 19.6 %collective-permute-start.32 = (bf16[3,192,1536]{2,1,0:T(8,128)(2,1)S(1)}, bf16[3,192,1536]{2,1,0:T(8,128)(2,1)S(1)}, u32[]{:S(2)}, u32[]{:S(2)}) collective-permute-start(bf16[3,192,1536]{2,1,0:T(8,128)(2,1)S(1)} %constant_dynamic-update-slice_fusion), channel_id=1, source_target_pairs={{0,1},{65,64},{2,3},{67,66},{4,5},{69,68},{6,7},{71,70},{8,9},{73,... | collective-permute-start | bytes 5308424 | tf_op jit(solution)/shard_map/ppermute | solution.py:513

commit v2 on v1

--- a/solution.py
+++ b/solution.py
@@ -61,10 +61,10 @@
         p = e * (1.0 / jnp.sum(e, axis=0, keepdims=True))
         delta = jnp.sum(p * dp, axis=0, keepdims=True)
         ds = (p * (dp - delta)).astype(BF)
-        dkv = dot(jnp.concatenate([ds, p.astype(BF)], axis=1), qd, 1, 0)
+        sides = jnp.concatenate([ds, p.astype(BF)], axis=1)
         for j in range(3):
             rows = slice((i + j) * tok, (i + j + 1) * tok)
-            part = dkv[j * tok : (j + 1) * tok]
+            part = dot(sides[j * tok : (j + 1) * tok], qd, 1, 0)
             if i == 0 or j == 2:
                 acc_ref[rows, :] = part
             else:
@@ -89,8 +89,10 @@
         low_ref[...] = held_ref[: D // 2, 2 * tok :]
         high_ref[...] = held_ref[D // 2 :, 2 * tok :]
 
-    grad_ref[:, : 2 * HEAD] = dot(held_ref[...], dkv_ref[...], 1, 0)
-    grad_ref[:, 2 * HEAD :] = dot(held_ref[...], dq_ref[...], 1, 0)
+    both = jnp.concatenate([dkv_ref[...], dq_ref[...]], axis=1)
+    for m in range(8):
+        part = slice(m * D // 8, (m + 1) * D // 8)
+        grad_ref[part, :] = dot(held_ref[part, :], both, 1, 0)
     fine = D // 8 // nz
     for out_ref, side in ((give_ref, 1 - place_ref[0]), (keep_ref, place_ref[0])):
         for steps in range(nz):

time: 231 us -> 229 us (level)
  no operation moved by 1% of the time
where the time goes in v2:
time: 229 us; the launch traced here: 228 us
  Pallas kernels  92.2 us (40%)
  starting transfers between devices  62.9 us (27%)
  waiting for transfers between devices  49.4 us (22%)
  other arithmetic  11.4 us (5%)
  local copies, waits for them, and re-layouts  11.1 us (5%)
    pallas_call x1, Pallas kernels, attention(): pl.pallas_call(lambda *refs: attention_kernel(tok, nz, *refs), grid_spec=...  32.6 us
    pallas_call x4, Pallas kernels, place_block(): pl.pallas_call(lambda *refs: place_kernel(split, *refs), grid_spec=pltpu....  26.5 us
    pallas_call x3, Pallas kernels, input_grads(): pl.pallas_call(input_kernel, grid_spec=pltpu.PrefetchScalarGridSpec(num_s...  19.1 us
    ppermute x1, waiting for transfers between devices, on_device(): other = lax.ppermute(result, ('xl', 'c'), [(0, 1), (3, 2)])  17.2 us
    ppermute x2, waiting for transfers between devices, swap_sides(): return lax.ppermute(value, ('xl', 'c'), [(1, 2), (2, 1)])  15.1 us
    ppermute x10, starting transfers between devices, side_ring(): return lax.ppermute(value, ('xl', axis, 'c'), pairs)  14.1 us
    ppermute x9, starting transfers between devices, ring(): lax.ppermute(value, axis, [(i, (i + steps) % count) for i in range(count)])  13 us
    ppermute x2, starting transfers between devices, swap_sides(): return lax.ppermute(value, ('xl', 'c'), [(1, 2), (2, 1)])  10.3 us
  transfers between devices with their start and end apart: 33, of which 11 were waited for; matrix products, arithmetic and copies ran while one was open for 7% of the time, Pallas kernels for 22%

profile of v2, /device:TPU:1, one launch (start us, length us, event | category | flops | bytes accessed | tf_op | source)
XLA Modules:
  0.0 228.3 jit_solution(6963367384898091789)
XLA Ops:
  0.6 4.5 %collective-permute-start = (bf16[384,1536]{1,0:T(8,128)(2,1)}, bf16[384,1536]{1,0:T(8,128)(2,1)}, u32[]{:S(2)}, u32[]{:S(2)}) collective-permute-start(bf16[384,1536]{1,0:T(8,128)(2,1)} %bitcast.68), channel_id=1, source_target_pairs={{1,64},{64,1},{3,66},{66,3},{5,68},{68,5},{7,70},{70,7},{9,72},{72... | collective-permute-start | bytes 3538952 | tf_op jit(solution)/shard_map/ppermute | solution.py:394
  5.2 1.7 collective-permute-start.1
  6.8 1.8 collective-permute-start.2
  8.6 4.9 %shard_map.84 = (bf16[1536,384]{1,0:T(8,128)(2,1)}, bf16[1536,768]{1,0:T(8,128)(2,1)}) custom-call(s32[1]{0:T(128)} %bitcast.place_ref, bf16[1536,1536]{1,0:T(8,128)(2,1)} %query_ref.1, bf16[1536,1536]{1,0:T(8,128)(2,1)} %key_ref.1, bf16[1536,1536]{1,0:T(8,128)(2,1)} %value_ref.1), custom_call_target="tpu_custom_call" | custom-call | flops 1099511627776 | bytes 7077888 | tf_op jit(solution)/shard_map/pallas_call | solution.py:152
  15.4 4.2 %collective-permute-done.refs_2_ = bf16[384,1536]{1,0:T(8,128)(2,1)} collective-permute-done((bf16[384,1536]{1,0:T(8,128)(2,1)}, bf16[384,1536]{1,0:T(8,128)(2,1)}, u32[]{:S(2)}, u32[]{:S(2)}) %collective-permute-start) | collective-permute-done | bytes 1179680 | tf_op jit(solution)/shard_map/ppermute | solution.py:394
  19.6 3.2 %collective-permute-start.7 = (bf16[384,1536]{1,0:T(8,128)(2,1)}, bf16[384,1536]{1,0:T(8,128)(2,1)}, u32[]{:S(2)}, u32[]{:S(2)}) collective-permute-start(bf16[384,1536]{1,0:T(8,128)(2,1)} %collective-permute-done.refs_2_), channel_id=1, source_target_pairs={{1,17},{17,33},{33,49},{49,1},{64,80},{80,96},{96,112},{112,64},{3... | collective-permute-start | bytes 3538952 | tf_op jit(solution)/shard_map/ppermute | solution.py:391
  22.8 3.4 %collective-permute-start.8 = (bf16[384,1536]{1,0:T(8,128)(2,1)}, bf16[384,1536]{1,0:T(8,128)(2,1)}, u32[]{:S(2)}, u32[]{:S(2)}) collective-permute-start(bf16[384,1536]{1,0:T(8,128)(2,1)} %collective-permute-done.refs_2_), channel_id=1, source_target_pairs={{1,49},{17,1},{33,17},{49,33},{64,112},{80,64},{96,80},{112,96},{3... | collective-permute-start | bytes 3538952 | tf_op jit(solution)/shard_map/ppermute | solution.py:391
  27.3 3.3 %collective-permute-start.3 = (bf16[384,384]{1,0:T(8,128)(2,1)}, bf16[384,384]{1,0:T(8,128)(2,1)}, u32[]{:S(2)}, u32[]{:S(2)}) collective-permute-start(bf16[384,384]{1,0:T(8,128)(2,1)} %get-tuple-element.126), channel_id=1, source_target_pairs={{0,32},{1,96},{16,48},{17,112},{32,0},{33,64},{48,16},{49,80},{64,... | collective-permute-start | bytes 884744 | tf_op jit(solution)/shard_map/ppermute | solution.py:407
  30.6 3.9 %collective-permute-start.5 = (bf16[384,384]{1,0:T(8,128)(2,1)}, bf16[384,384]{1,0:T(8,128)(2,1)}, u32[]{:S(2)}, u32[]{:S(2)}) collective-permute-start(bf16[384,384]{1,0:T(8,128)(2,1)} %get-tuple-element.124), channel_id=1, source_target_pairs={{0,48},{1,112},{16,0},{17,64},{32,16},{33,80},{48,32},{49,96},{64,... | collective-permute-start | bytes 884744 | tf_op jit(solution)/shard_map/ppermute | solution.py:407
  34.5 6.8 %shard_map.85 = (bf16[1536,1536]{1,0:T(8,128)(2,1)}, bf16[1536,768]{1,0:T(8,128)(2,1)}, bf16[1536,384]{1,0:T(8,128)(2,1)}) custom-call(s32[2]{0:T(128)} %pad_add_fusion.2.refs_0_, bf16[384,1536]{1,0:T(8,128)(2,1)} %bitcast.71, bf16[384,1536]{1,0:T(8,128)(2,1)} %collective-permute-done.refs_2_, bf16[1536,768]{1,0:T(8,128)(2,1)} %get-tuple-element.66.refs_3_.wkv_ref, ...), custom_call_target="tpu_custom_call" | custom-call | flops 1099511627776 | bytes 4718592 | tf_op jit(solution)/shard_map/pallas_call | solution.py:234
  41.3 1.9 collective-permute-start.6
  44.4 1.7 constant_dynamic-update-slice_fusion.6
  46.1 1.7 constant_dynamic-update-slice_fusion.5
  47.8 1.7 constant_dynamic-update-slice_fusion.4
  49.8 1.7 select_dynamic-update-slice_fusion.refs_5_
  51.5 1.2 collective-permute-done.8.right_away.refs_2_
  52.8 2.5 %shard_map.86 = (bf16[192,1536]{1,0:T(8,128)(2,1)}, bf16[192,1536]{1,0:T(8,128)(2,1)}) custom-call(s32[1]{0:T(128)} %bitcast.5.place_ref, bf16[384,1536]{1,0:T(8,128)(2,1)} %collective-permute-done.1.left_home.refs_1_, bf16[384,1536]{1,0:T(8,128)(2,1)} %collective-permute-done.7.left_away.refs_2_, ...), custom_call_target="tpu_custom_call" | custom-call | flops 294912 | bytes 3538944 | tf_op jit(solution)/shard_map/pallas_call | solution.py:189
  55.2 2.7 %collective-permute-start.10 = (bf16[192,1536]{1,0:T(8,128)(2,1)}, bf16[192,1536]{1,0:T(8,128)(2,1)}, u32[]{:S(2)}, u32[]{:S(2)}) collective-permute-start(bf16[192,1536]{1,0:T(8,128)(2,1)} %get-tuple-element.76), channel_id=1, source_target_pairs={{0,48},{16,0},{32,16},{48,32},{1,49},{17,1},{33,17},{49,33},{2,50}... | collective-permute-start | bytes 1769480 | tf_op jit(solution)/shard_map/ppermute | solution.py:382
  57.9 6.7 %shard_map.87 = (bf16[1536,1536]{1,0:T(8,128)(2,1)}, bf16[1536,768]{1,0:T(8,128)(2,1)}, bf16[1536,384]{1,0:T(8,128)(2,1)}) custom-call(s32[2]{0:T(128)} %pad_add_fusion.5.refs_0_, bf16[384,1536]{1,0:T(8,128)(2,1)} %collective-permute-done.1.left_home.refs_1_, ...), custom_call_target="tpu_custom_call", output_to_operand_aliasing={{0}: (5, {}), {1}: (6, {}), {2}: (7, {})} | custom-call | flops 1099511627776 | bytes 4718592 | tf_op jit(solution)/shard_map/pallas_call | solution.py:234
  64.6 6.7 %shard_map.88 = (bf16[1536,1536]{1,0:T(8,128)(2,1)}, bf16[1536,768]{1,0:T(8,128)(2,1)}, bf16[1536,384]{1,0:T(8,128)(2,1)}) custom-call(s32[2]{0:T(128)} %get-tuple-element.168.refs_0_, bf16[384,1536]{1,0:T(8,128)(2,1)} %collective-permute-done.2.right_home.refs_1_, ...), custom_call_target="tpu_custom_call", output_to_operand_aliasing={{0}: (5, {}), {1}: (6, {}), {2}: (7, {})} | custom-call | flops 1099511627776 | bytes 4718592 | tf_op jit(solution)/shard_map/pallas_call | solution.py:234
  71.3 6.2 %shard_map.89 = (bf16[1536,1536]{1,0:T(8,128)(2,1)}, bf16[1536,768]{1,0:T(8,128)(2,1)}, bf16[1536,384]{1,0:T(8,128)(2,1)}) custom-call(s32[2]{0:T(128)} %get-tuple-element.167.refs_0_, bf16[192,1536]{1,0:T(8,128)(2,1)} %collective-permute-done.9.refs_1_, ...), custom_call_target="tpu_custom_call", output_to_operand_aliasing={{0}: (5, {}), {1}: (6, {}), {2}: (7, {})} | custom-call | flops 1099511627776 | bytes 4718592 | tf_op jit(solution)/shard_map/pallas_call | solution.py:234
  77.5 1.3 slice.129
  78.9 1.5 collective-permute-start.11
  81.0 5.4 %collective-permute-done.11.refs_4_ = bf16[768,768]{1,0:T(8,128)(2,1)S(1)} collective-permute-done((bf16[768,768]{1,0:T(8,128)(2,1)S(1)}, bf16[768,768]{1,0:T(8,128)(2,1)S(1)}, u32[]{:S(2)}, u32[]{:S(2)}) %collective-permute-start.11) | collective-permute-done | bytes 1179680 | tf_op jit(solution)/shard_map/ppermute | solution.py:441
  87.4 32.6 %shard_map.90 = (bf16[1536,384]{1,0:T(8,128)(2,1)}, bf16[1536,768]{1,0:T(8,128)(2,1)}, bf16[768,768]{1,0:T(8,128)(2,1)}, bf16[4,4,48,1152]{3,2,1,0:T(8,128)(2,1)...) custom-call(s32[2]{0:T(128)} %pad_add_fusion.refs_0_, ...), custom_call_target="tpu_custom_call" | custom-call | flops 19025362944 | bytes 28311552 | tf_op jit(solution)/shard_map/pallas_call | solution.py:114
  120.0 2.1 collective-permute-start.12
  122.8 1.3 collective-permute-start.14
  125.7 5.1 %shard_map.91 = (bf16[192,1536]{1,0:T(8,128)(2,1)}, bf16[192,1536]{1,0:T(8,128)(2,1)}) custom-call(s32[1]{0:T(128)} %bitcast.4.place_ref, bf16[1536,768]{1,0:T(8,128)(2,1)} %get-tuple-element.110.dkv_ref, bf16[768,768]{1,0:T(8,128)(2,1)} %copy-done.2, bf16[1536,384]{1,0:T(8,128)(2,1)} %get-tuple-element.93.dq_ref, ...), custom_call_target="tpu_custom_call" | custom-call | flops 1099511627776 | bytes 12582912 | tf_op jit(solution)/shard_map/pallas_call | solution.py:342
  130.8 1.9 collective-permute-start.18
  132.8 6.7 %shard_map.92 = (bf16[4,48,1152]{2,1,0:T(8,128)(2,1)}, bf16[4,48,1152]{2,1,0:T(8,128)(2,1)}, bf16[4,48,1152]{2,1,0:T(8,128)(2,1)}, bf16[4,48,1152]{2,1,0:T(8,128)(2,1)}) custom-call(s32[2]{0:T(128)} %pad_add_fusion.refs_0_, bf16[4,4,48,1152]{3,2,1,0:T(8,128)(2,1)} %get-tuple-element.96.refs_1_, bf16[4,4,48,1152]{3,2,1,0:T(8,128)(2,1)} %collective-permute-done.13.refs_2_, ...), custom_call_target="tpu_custom_call" | custom-call | flops 1099511627776 | bytes 12582912 | tf_op jit(solution)/shard_map/pallas_call | solution.py:292
  139.5 1.7 collective-permute-start.15
  141.2 3.3 %collective-permute-start.16 = (bf16[4,48,1152]{2,1,0:T(8,128)(2,1)}, bf16[4,48,1152]{2,1,0:T(8,128)(2,1)}, u32[]{:S(2)}, u32[]{:S(2)}) collective-permute-start(bf16[4,48,1152]{2,1,0:T(8,128)(2,1)} %get-tuple-element.104), channel_id=1, source_target_pairs={{0,4},{2,6},{4,0},{6,2},{1,5},{3,7},{5,1},{7,3},{8,12},{10,14},{12... | collective-permute-start | bytes 1327112 | tf_op jit(solution)/shard_map/ppermute | solution.py:382
  145.2 2.1 collective-permute-done.19.refs_1_
  147.3 8.8 %shard_map.93 = (bf16[384,1536]{1,0:T(8,128)(2,1)}, bf16[384,1536]{1,0:T(8,128)(2,1)}) custom-call(s32[2]{0:T(128)} %pad_add_fusion.4.place_ref, bf16[1536,768]{1,0:T(8,128)(2,1)} %get-tuple-element.110.dkv_ref, bf16[768,768]{1,0:T(8,128)(2,1)} %copy-done.2, bf16[1536,384]{1,0:T(8,128)(2,1)} %get-tuple-element.93.dq_ref, ...), custom_call_target="tpu_custom_call" | custom-call | flops 1099511627776 | bytes 12582912 | tf_op jit(solution)/shard_map/pallas_call | solution.py:342
  156.1 2.7 %collective-permute-start.24 = (bf16[384,1536]{1,0:T(8,128)(2,1)}, bf16[384,1536]{1,0:T(8,128)(2,1)S(1)}, u32[]{:S(2)}, u32[]{:S(2)}) collective-permute-start(bf16[384,1536]{1,0:T(8,128)(2,1)} %get-tuple-element.106), channel_id=1, source_target_pairs={{0,48},{16,0},{32,16},{48,32},{1,49},{17,1},{33,17},{49,33},{2,50}... | collective-permute-start | bytes 3538952 | tf_op jit(solution)/shard_map/ppermute | solution.py:382
  158.7 3.9 %collective-permute-done.16 = bf16[4,48,1152]{2,1,0:T(8,128)(2,1)} collective-permute-done((bf16[4,48,1152]{2,1,0:T(8,128)(2,1)}, bf16[4,48,1152]{2,1,0:T(8,128)(2,1)}, u32[]{:S(2)}, u32[]{:S(2)}) %collective-permute-start.16) | collective-permute-done | bytes 442400 | tf_op jit(solution)/shard_map/ppermute | solution.py:382
  163.4 1.5 add_convert_fusion.2
  164.9 5.7 %collective-permute-start.20 = (bf16[4,48,1152]{2,1,0:T(8,128)(2,1)S(1)}, bf16[4,48,1152]{2,1,0:T(8,128)(2,1)S(1)}, u32[]{:S(2)}, u32[]{:S(2)}) collective-permute-start(bf16[4,48,1152]{2,1,0:T(8,128)(2,1)S(1)} %add_convert_fusion.2), channel_id=1, source_target_pairs={{64,0},{72,8},{9,65},{1,73},{66,2},{74,10},{11,67},{3,75},{68,4},{... | collective-permute-start | bytes 1327112 | tf_op jit(solution)/shard_map/ppermute | solution.py:485
  170.6 1.4 collective-permute-start.21
  172.0 3.1 %collective-permute-start.22 = (bf16[4,48,1152]{2,1,0:T(8,128)(2,1)S(1)}, bf16[4,48,1152]{2,1,0:T(8,128)(2,1)}, u32[]{:S(2)}, u32[]{:S(2)}) collective-permute-start(bf16[4,48,1152]{2,1,0:T(8,128)(2,1)S(1)} %add_convert_fusion.2), channel_id=1, source_target_pairs={{72,0},{64,8},{1,65},{9,73},{74,2},{66,10},{3,67},{11,75},{76,4},{... | collective-permute-start | bytes 1327112 | tf_op jit(solution)/shard_map/ppermute | solution.py:485
  175.1 5.2 %shard_map.94 = bf16[384,1536]{1,0:T(8,128)(2,1)} custom-call(s32[1]{0:T(128)} %bitcast.place_ref, bf16[1536,768]{1,0:T(8,128)(2,1)} %get-tuple-element.110.dkv_ref, bf16[768,768]{1,0:T(8,128)(2,1)} %copy-done.2, bf16[1536,384]{1,0:T(8,128)(2,1)} %get-tuple-element.93.dq_ref, bf16[1536,768]{1,0:T(8,128)(2,1)} %get-tuple-element.66.refs_3_.wkv_ref, ...), custom_call_target="tpu_custom_call" | custom-call | flops 1358954496 | bytes 12582912 | tf_op jit(solution)/shard_map/pallas_call | solution.py:342
  180.3 2.9 %collective-permute-done.22 = bf16[4,48,1152]{2,1,0:T(8,128)(2,1)} collective-permute-done((bf16[4,48,1152]{2,1,0:T(8,128)(2,1)S(1)}, bf16[4,48,1152]{2,1,0:T(8,128)(2,1)}, u32[]{:S(2)}, u32[]{:S(2)}) %collective-permute-start.22) | collective-permute-done | bytes 442400 | tf_op jit(solution)/shard_map/ppermute | solution.py:485
  183.2 1.4 add_convert_fusion.1
  187.2 5.8 %collective-permute-start.31 = (bf16[384,1536]{1,0:T(8,128)(2,1)S(1)}, bf16[384,1536]{1,0:T(8,128)(2,1)S(1)}, u32[]{:S(2)}, u32[]{:S(2)}) collective-permute-start(bf16[384,1536]{1,0:T(8,128)(2,1)S(1)} %add_convert_fusion), channel_id=1, source_target_pairs={{1,64},{64,1},{3,66},{66,3},{5,68},{68,5},{7,70},{70,7},{9,72},{72... | collective-permute-start | bytes 3538952 | tf_op jit(solution)/shard_map/ppermute | solution.py:394
  195.9 10.9 %collective-permute-done.31 = bf16[384,1536]{1,0:T(8,128)(2,1)S(1)} collective-permute-done((bf16[384,1536]{1,0:T(8,128)(2,1)S(1)}, bf16[384,1536]{1,0:T(8,128)(2,1)S(1)}, u32[]{:S(2)}, u32[]{:S(2)}) %collective-permute-start.31) | collective-permute-done | bytes 1179680 | tf_op jit(solution)/shard_map/ppermute | solution.py:394
  206.8 1.3 collective-permute-start.32
  209.2 17.2 %collective-permute-done.32 = bf16[3,192,1536]{2,1,0:T(8,128)(2,1)S(1)} collective-permute-done((bf16[3,192,1536]{2,1,0:T(8,128)(2,1)S(1)}, bf16[3,192,1536]{2,1,0:T(8,128)(2,1)S(1)}, u32[]{:S(2)}, u32[]{:S(2)}) %collective-permute-start.32) | collective-permute-done | bytes 1769504 | tf_op jit(solution)/shard_map/ppermute | solution.py:515
  226.4 1.9 fusion.1
  (85 shorter events, 16.2 us)
Async XLA Ops:
  0.6 19.0 %collective-permute-start = (bf16[384,1536]{1,0:T(8,128)(2,1)}, bf16[384,1536]{1,0:T(8,128)(2,1)}, u32[]{:S(2)}, u32[]{:S(2)}) collective-permute-start(bf16[384,1536]{1,0:T(8,128)(2,1)} %bitcast.68), channel_id=1, source_target_pairs={{1,64},{64,1},{3,66},{66,3},{5,68},{68,5},{7,70},{70,7},{9,72},{72... | collective-permute-start | bytes 3538952 | tf_op jit(solution)/shard_map/ppermute | solution.py:394
  5.2 14.5 %collective-permute-start.1 = (bf16[384,1536]{1,0:T(8,128)(2,1)}, bf16[384,1536]{1,0:T(8,128)(2,1)}, u32[]{:S(2)}, u32[]{:S(2)}) collective-permute-start(bf16[384,1536]{1,0:T(8,128)(2,1)} %bitcast.69), channel_id=1, source_target_pairs={{0,16},{16,32},{32,48},{48,0},{65,81},{81,97},{97,113},{113,65},{2... | collective-permute-start | bytes 3538952 | tf_op jit(solution)/shard_map/ppermute | solution.py:391
  6.8 12.8 %collective-permute-start.2 = (bf16[384,1536]{1,0:T(8,128)(2,1)}, bf16[384,1536]{1,0:T(8,128)(2,1)}, u32[]{:S(2)}, u32[]{:S(2)}) collective-permute-start(bf16[384,1536]{1,0:T(8,128)(2,1)} %bitcast.70), channel_id=1, source_target_pairs={{0,48},{16,0},{32,16},{48,32},{65,113},{81,65},{97,81},{113,97},{2... | collective-permute-start | bytes 3538952 | tf_op jit(solution)/shard_map/ppermute | solution.py:391
  8.6 17.6 %copy-start.1 = (bf16[1,384,1536]{2,1,0:T(8,128)(2,1)S(1)}, bf16[1,384,1536]{2,1,0:T(8,128)(2,1)}, u32[]{:S(2)}) copy-start(bf16[1,384,1536]{2,1,0:T(8,128)(2,1)} %param.9) | copy-start | bytes 3538948
  19.6 31.9 %collective-permute-start.7 = (bf16[384,1536]{1,0:T(8,128)(2,1)}, bf16[384,1536]{1,0:T(8,128)(2,1)}, u32[]{:S(2)}, u32[]{:S(2)}) collective-permute-start(bf16[384,1536]{1,0:T(8,128)(2,1)} %collective-permute-done.refs_2_), channel_id=1, source_target_pairs={{1,17},{17,33},{33,49},{49,1},{64,80},{80,96},{96,112},{112,64},{3... | collective-permute-start | bytes 3538952 | tf_op jit(solution)/shard_map/ppermute | solution.py:391
  22.8 29.9 %collective-permute-start.8 = (bf16[384,1536]{1,0:T(8,128)(2,1)}, bf16[384,1536]{1,0:T(8,128)(2,1)}, u32[]{:S(2)}, u32[]{:S(2)}) collective-permute-start(bf16[384,1536]{1,0:T(8,128)(2,1)} %collective-permute-done.refs_2_), channel_id=1, source_target_pairs={{1,49},{17,1},{33,17},{49,33},{64,112},{80,64},{96,80},{112,96},{3... | collective-permute-start | bytes 3538952 | tf_op jit(solution)/shard_map/ppermute | solution.py:391
  27.3 14.0 %collective-permute-start.3 = (bf16[384,384]{1,0:T(8,128)(2,1)}, bf16[384,384]{1,0:T(8,128)(2,1)}, u32[]{:S(2)}, u32[]{:S(2)}) collective-permute-start(bf16[384,384]{1,0:T(8,128)(2,1)} %get-tuple-element.126), channel_id=1, source_target_pairs={{0,32},{1,96},{16,48},{17,112},{32,0},{33,64},{48,16},{49,80},{64,... | collective-permute-start | bytes 884744 | tf_op jit(solution)/shard_map/ppermute | solution.py:407
  30.6 15.5 %collective-permute-start.4 = (bf16[384,384]{1,0:T(8,128)(2,1)}, bf16[384,384]{1,0:T(8,128)(2,1)}, u32[]{:S(2)}, u32[]{:S(2)}) collective-permute-start(bf16[384,384]{1,0:T(8,128)(2,1)} %get-tuple-element.125), channel_id=1, source_target_pairs={{0,16},{1,80},{16,32},{17,96},{32,48},{33,112},{48,0},{49,64},{64,... | collective-permute-start | bytes 884744 | tf_op jit(solution)/shard_map/ppermute | solution.py:407
  30.6 17.2 %collective-permute-start.5 = (bf16[384,384]{1,0:T(8,128)(2,1)}, bf16[384,384]{1,0:T(8,128)(2,1)}, u32[]{:S(2)}, u32[]{:S(2)}) collective-permute-start(bf16[384,384]{1,0:T(8,128)(2,1)} %get-tuple-element.124), channel_id=1, source_target_pairs={{0,48},{1,112},{16,0},{17,64},{32,16},{33,80},{48,32},{49,96},{64,... | collective-permute-start | bytes 884744 | tf_op jit(solution)/shard_map/ppermute | solution.py:407
  34.5 6.8 %copy-start.4 = (bf16[384,384]{1,0:T(8,128)(2,1)S(1)}, bf16[384,384]{1,0:T(8,128)(2,1)}, u32[]{:S(2)}) copy-start(bf16[384,384]{1,0:T(8,128)(2,1)} %get-tuple-element.123) | copy-start | bytes 884740
  41.3 8.4 %collective-permute-start.6 = (bf16[384,384]{1,0:T(8,128)(2,1)S(1)}, bf16[384,384]{1,0:T(8,128)(2,1)S(1)}, u32[]{:S(2)}, u32[]{:S(2)}) collective-permute-start(bf16[384,384]{1,0:T(8,128)(2,1)S(1)} %copy-done.4), channel_id=1, source_target_pairs={{1,64},{17,80},{33,96},{49,112},{64,1},{80,17},{96,33},{112,49},{3... | collective-permute-start | bytes 884744 | tf_op jit(solution)/shard_map/ppermute | solution.py:407
  55.2 16.1 %collective-permute-start.10 = (bf16[192,1536]{1,0:T(8,128)(2,1)}, bf16[192,1536]{1,0:T(8,128)(2,1)}, u32[]{:S(2)}, u32[]{:S(2)}) collective-permute-start(bf16[192,1536]{1,0:T(8,128)(2,1)} %get-tuple-element.76), channel_id=1, source_target_pairs={{0,48},{16,0},{32,16},{48,32},{1,49},{17,1},{33,17},{49,33},{2,50}... | collective-permute-start | bytes 1769480 | tf_op jit(solution)/shard_map/ppermute | solution.py:382
  57.9 13.4 %collective-permute-start.9 = (bf16[192,1536]{1,0:T(8,128)(2,1)}, bf16[192,1536]{1,0:T(8,128)(2,1)}, u32[]{:S(2)}, u32[]{:S(2)}) collective-permute-start(bf16[192,1536]{1,0:T(8,128)(2,1)} %get-tuple-element.75), channel_id=1, source_target_pairs={{0,16},{16,32},{32,48},{48,0},{1,17},{17,33},{33,49},{49,1},{2,18}... | collective-permute-start | bytes 1769480 | tf_op jit(solution)/shard_map/ppermute | solution.py:382
  78.9 7.5 %collective-permute-start.11 = (bf16[768,768]{1,0:T(8,128)(2,1)S(1)}, bf16[768,768]{1,0:T(8,128)(2,1)S(1)}, u32[]{:S(2)}, u32[]{:S(2)}) collective-permute-start(bf16[768,768]{1,0:T(8,128)(2,1)S(1)} %slice.129), channel_id=1, source_target_pairs={{0,1},{2,3},{4,5},{6,7},{8,9},{10,11},{12,13},{14,15},{16,17},{18,... | collective-permute-start | bytes 3538952 | tf_op jit(solution)/shard_map/ppermute | solution.py:441
  86.4 1.0 copy-start.5
  120.0 4.7 %collective-permute-start.12 = (bf16[768,768]{1,0:T(8,128)(2,1)}, bf16[768,768]{1,0:T(8,128)(2,1)S(1)}, u32[]{:S(2)}, u32[]{:S(2)}) collective-permute-start(bf16[768,768]{1,0:T(8,128)(2,1)} %get-tuple-element.92.refs_5_), channel_id=1, source_target_pairs={{1,0},{3,2},{5,4},{7,6},{9,8},{11,10},{13,12},{15,14},{17,16},{19,... | collective-permute-start | bytes 3538952 | tf_op jit(solution)/shard_map/ppermute | solution.py:447
  122.8 10.0 %collective-permute-start.13 = (bf16[4,4,48,1152]{3,2,1,0:T(8,128)(2,1)}, bf16[4,4,48,1152]{3,2,1,0:T(8,128)(2,1)}, u32[]{:S(2)}, u32[]{:S(2)}) collective-permute-start(bf16[4,4,48,1152]{3,2,1,0:T(8,128)(2,1)} %get-tuple-element.97), channel_id=1, source_target_pairs={{0,1},{1,0},{2,3},{3,2},{4,5},{5,4},{6,7},{7,6},{8,9},{9,8},{10,11... | collective-permute-start | bytes 5308424 | tf_op jit(solution)/shard_map/ppermute | solution.py:448
  122.8 10.0 %collective-permute-start.14 = (bf16[768,768]{1,0:T(8,128)(2,1)}, bf16[768,768]{1,0:T(8,128)(2,1)}, u32[]{:S(2)}, u32[]{:S(2)}) collective-permute-start(bf16[768,768]{1,0:T(8,128)(2,1)} %get-tuple-element.99), channel_id=1, source_target_pairs={{0,1},{2,3},{4,5},{6,7},{8,9},{10,11},{12,13},{14,15},{16,17},{18,... | collective-permute-start | bytes 3538952 | tf_op jit(solution)/shard_map/ppermute | solution.py:449
  124.7 1.0 copy-start.2
  130.8 14.4 %collective-permute-start.18 = (bf16[192,1536]{1,0:T(8,128)(2,1)}, bf16[192,1536]{1,0:T(8,128)(2,1)}, u32[]{:S(2)}, u32[]{:S(2)}) collective-permute-start(bf16[192,1536]{1,0:T(8,128)(2,1)} %get-tuple-element.94), channel_id=1, source_target_pairs={{0,48},{16,0},{32,16},{48,32},{1,49},{17,1},{33,17},{49,33},{2,50}... | collective-permute-start | bytes 1769480 | tf_op jit(solution)/shard_map/ppermute | solution.py:382
  132.8 14.5 %collective-permute-start.19 = (bf16[192,1536]{1,0:T(8,128)(2,1)}, bf16[192,1536]{1,0:T(8,128)(2,1)}, u32[]{:S(2)}, u32[]{:S(2)}) collective-permute-start(bf16[192,1536]{1,0:T(8,128)(2,1)} %get-tuple-element.95), channel_id=1, source_target_pairs={{0,16},{16,32},{32,48},{48,0},{1,17},{17,33},{33,49},{49,1},{2,18}... | collective-permute-start | bytes 1769480 | tf_op jit(solution)/shard_map/ppermute | solution.py:382
  139.5 19.3 %collective-permute-start.15 = (bf16[4,48,1152]{2,1,0:T(8,128)(2,1)}, bf16[4,48,1152]{2,1,0:T(8,128)(2,1)}, u32[]{:S(2)}, u32[]{:S(2)}) collective-permute-start(bf16[4,48,1152]{2,1,0:T(8,128)(2,1)} %get-tuple-element.103), channel_id=1, source_target_pairs={{0,2},{2,4},{4,6},{6,0},{1,3},{3,5},{5,7},{7,1},{8,10},{10,12},{12... | collective-permute-start | bytes 1327112 | tf_op jit(solution)/shard_map/ppermute | solution.py:382
  141.2 21.4 %collective-permute-start.16 = (bf16[4,48,1152]{2,1,0:T(8,128)(2,1)}, bf16[4,48,1152]{2,1,0:T(8,128)(2,1)}, u32[]{:S(2)}, u32[]{:S(2)}) collective-permute-start(bf16[4,48,1152]{2,1,0:T(8,128)(2,1)} %get-tuple-element.104), channel_id=1, source_target_pairs={{0,4},{2,6},{4,0},{6,2},{1,5},{3,7},{5,1},{7,3},{8,12},{10,14},{12... | collective-permute-start | bytes 1327112 | tf_op jit(solution)/shard_map/ppermute | solution.py:382
  144.5 18.9 %collective-permute-start.17 = (bf16[4,48,1152]{2,1,0:T(8,128)(2,1)}, bf16[4,48,1152]{2,1,0:T(8,128)(2,1)}, u32[]{:S(2)}, u32[]{:S(2)}) collective-permute-start(bf16[4,48,1152]{2,1,0:T(8,128)(2,1)} %get-tuple-element.105), channel_id=1, source_target_pairs={{0,6},{2,0},{4,2},{6,4},{1,7},{3,1},{5,3},{7,5},{8,14},{10,8},{12,... | collective-permute-start | bytes 1327112 | tf_op jit(solution)/shard_map/ppermute | solution.py:382
  147.3 16.1 %copy-start.3 = (bf16[4,48,1152]{2,1,0:T(8,128)(2,1)S(1)}, bf16[4,48,1152]{2,1,0:T(8,128)(2,1)}, u32[]{:S(2)}) copy-start(bf16[4,48,1152]{2,1,0:T(8,128)(2,1)} %get-tuple-element.102) | copy-start | bytes 1327108
  156.1 27.2 %collective-permute-start.23 = (bf16[384,1536]{1,0:T(8,128)(2,1)}, bf16[384,1536]{1,0:T(8,128)(2,1)S(1)}, u32[]{:S(2)}, u32[]{:S(2)}) collective-permute-start(bf16[384,1536]{1,0:T(8,128)(2,1)} %get-tuple-element.112), channel_id=1, source_target_pairs={{0,16},{16,32},{32,48},{48,0},{1,17},{17,33},{33,49},{49,1},{2,18}... | collective-permute-start | bytes 3538952 | tf_op jit(solution)/shard_map/ppermute | solution.py:382
  156.1 27.2 %collective-permute-start.24 = (bf16[384,1536]{1,0:T(8,128)(2,1)}, bf16[384,1536]{1,0:T(8,128)(2,1)S(1)}, u32[]{:S(2)}, u32[]{:S(2)}) collective-permute-start(bf16[384,1536]{1,0:T(8,128)(2,1)} %get-tuple-element.106), channel_id=1, source_target_pairs={{0,48},{16,0},{32,16},{48,32},{1,49},{17,1},{33,17},{49,33},{2,50}... | collective-permute-start | bytes 3538952 | tf_op jit(solution)/shard_map/ppermute | solution.py:382
  164.9 15.5 %collective-permute-start.20 = (bf16[4,48,1152]{2,1,0:T(8,128)(2,1)S(1)}, bf16[4,48,1152]{2,1,0:T(8,128)(2,1)S(1)}, u32[]{:S(2)}, u32[]{:S(2)}) collective-permute-start(bf16[4,48,1152]{2,1,0:T(8,128)(2,1)S(1)} %add_convert_fusion.2), channel_id=1, source_target_pairs={{64,0},{72,8},{9,65},{1,73},{66,2},{74,10},{11,67},{3,75},{68,4},{... | collective-permute-start | bytes 1327112 | tf_op jit(solution)/shard_map/ppermute | solution.py:485
  170.6 9.8 %collective-permute-start.21 = (bf16[4,48,1152]{2,1,0:T(8,128)(2,1)S(1)}, bf16[4,48,1152]{2,1,0:T(8,128)(2,1)}, u32[]{:S(2)}, u32[]{:S(2)}) collective-permute-start(bf16[4,48,1152]{2,1,0:T(8,128)(2,1)S(1)} %add_convert_fusion.2), channel_id=1, source_target_pairs={{8,0},{0,8},{73,65},{65,73},{10,2},{2,10},{75,67},{67,75},{12,4},{... | collective-permute-start | bytes 1327112 | tf_op jit(solution)/shard_map/ppermute | solution.py:485
  172.0 11.2 %collective-permute-start.22 = (bf16[4,48,1152]{2,1,0:T(8,128)(2,1)S(1)}, bf16[4,48,1152]{2,1,0:T(8,128)(2,1)}, u32[]{:S(2)}, u32[]{:S(2)}) collective-permute-start(bf16[4,48,1152]{2,1,0:T(8,128)(2,1)S(1)} %add_convert_fusion.2), channel_id=1, source_target_pairs={{72,0},{64,8},{1,65},{9,73},{74,2},{66,10},{3,67},{11,75},{76,4},{... | collective-permute-start | bytes 1327112 | tf_op jit(solution)/shard_map/ppermute | solution.py:485
  180.3 6.4 %copy-start = (bf16[384,1536]{1,0:T(8,128)(2,1)S(1)}, bf16[384,1536]{1,0:T(8,128)(2,1)}, u32[]{:S(2)}) copy-start(bf16[384,1536]{1,0:T(8,128)(2,1)} %shard_map.94) | copy-start | bytes 3538948
  184.7 8.4 %collective-permute-start.27 = (bf16[48,1152]{1,0:T(8,128)(2,1)S(1)}, bf16[48,1152]{1,0:T(8,128)(2,1)S(1)}, u32[]{:S(2)}, u32[]{:S(2)}) collective-permute-start(bf16[48,1152]{1,0:T(8,128)(2,1)S(1)} %get-tuple-element.127), channel_id=1, source_target_pairs={{0,48},{16,0},{32,16},{48,32},{65,113},{81,65},{97,81},{113,97},{2... | collective-permute-start | bytes 331784 | tf_op jit(solution)/shard_map/ppermute | solution.py:391
  185.3 7.8 %collective-permute-start.26 = (bf16[48,1152]{1,0:T(8,128)(2,1)S(1)}, bf16[48,1152]{1,0:T(8,128)(2,1)S(1)}, u32[]{:S(2)}, u32[]{:S(2)}) collective-permute-start(bf16[48,1152]{1,0:T(8,128)(2,1)S(1)} %get-tuple-element.128), channel_id=1, source_target_pairs={{0,32},{16,48},{32,0},{48,16},{65,97},{81,113},{97,65},{113,81},{2... | collective-permute-start | bytes 331784 | tf_op jit(solution)/shard_map/ppermute | solution.py:391
  186.0 7.2 %collective-permute-start.25 = (bf16[48,1152]{1,0:T(8,128)(2,1)S(1)}, bf16[48,1152]{1,0:T(8,128)(2,1)S(1)}, u32[]{:S(2)}, u32[]{:S(2)}) collective-permute-start(bf16[48,1152]{1,0:T(8,128)(2,1)S(1)} %get-tuple-element.129), channel_id=1, source_target_pairs={{0,16},{16,32},{32,48},{48,0},{65,81},{81,97},{97,113},{113,65},{2... | collective-permute-start | bytes 331784 | tf_op jit(solution)/shard_map/ppermute | solution.py:391
  187.2 19.6 %collective-permute-start.31 = (bf16[384,1536]{1,0:T(8,128)(2,1)S(1)}, bf16[384,1536]{1,0:T(8,128)(2,1)S(1)}, u32[]{:S(2)}, u32[]{:S(2)}) collective-permute-start(bf16[384,1536]{1,0:T(8,128)(2,1)S(1)} %add_convert_fusion), channel_id=1, source_target_pairs={{1,64},{64,1},{3,66},{66,3},{5,68},{68,5},{7,70},{70,7},{9,72},{72... | collective-permute-start | bytes 3538952 | tf_op jit(solution)/shard_map/ppermute | solution.py:394
  193.4 2.3 %collective-permute-start.28 = (bf16[3,48,1536]{2,1,0:T(8,128)(2,1)S(1)}, bf16[3,48,1536]{2,1,0:T(8,128)(2,1)S(1)}, u32[]{:S(2)}, u32[]{:S(2)}) collective-permute-start(bf16[3,48,1536]{2,1,0:T(8,128)(2,1)S(1)} %maximum_dynamic-update-slice_fusion.3), channel_id=1, source_target_pairs={{0,2},{2,4},{4,6},{6,0},{65,67},{67,69},{69,71},{71,65},{8,10},{10... | collective-permute-start | bytes 1327112 | tf_op jit(solution)/shard_map/ppermute | solution.py:391
  194.2 1.6 collective-permute-start.29
  194.9 1.0 collective-permute-start.30
  206.8 19.6 %collective-permute-start.32 = (bf16[3,192,1536]{2,1,0:T(8,128)(2,1)S(1)}, bf16[3,192,1536]{2,1,0:T(8,128)(2,1)S(1)}, u32[]{:S(2)}, u32[]{:S(2)}) collective-permute-start(bf16[3,192,1536]{2,1,0:T(8,128)(2,1)S(1)} %constant_dynamic-update-slice_fusion), channel_id=1, source_target_pairs={{0,1},{65,64},{2,3},{67,66},{4,5},{69,68},{6,7},{71,70},{8,9},{73,... | collective-permute-start | bytes 5308424 | tf_op jit(solution)/shard_map/ppermute | solution.py:515
